TPU v7x, 32 devices: a whole 2x2x4 slice. The times are simulated.
32 devices in a mesh: dp: 8 (over y, x, core), mp: 4 (over z).
Axes of the slice: x: 2, y: 2, z: 4, core: 2. Of those that a mesh axis runs over, the one named last changes fastest.
Arguments:
- hidden_in: bfloat16 [16384, 768], P(('dp', 'mp')), may hold values from -6 to 6
- lengths: int32 [8, 3], P('dp'), may hold values from 1 to 1664, as said below
- w_qkv: float32 [3, 768, 768], P(None, 'dp', 'mp'), may hold values from -0.21875 to 0.21875
- b_qv: float32 [2, 768], P(None, ('dp', 'mp')), may hold values from -1.75 to 1.75
- w_out: float32 [768, 768], P('mp', 'dp'), may hold values from -0.875 to 0.875
- b_out: float32 [768], P(('dp', 'mp')), may hold values from -1.75 to 1.75
- ln1_gain: float32 [768], P(('dp', 'mp')), may hold values from 0.1 to 1.9
- ln1_bias: float32 [768], P(('dp', 'mp')), may hold values from -1.75 to 1.75
- w_gu: float32 [2, 768, 3072], P(None, 'dp', 'mp'), may hold values from -0.21875 to 0.21875
- b_gu: float32 [2, 3072], P(None, ('dp', 'mp')), may hold values from -1.75 to 1.75
- w_down: float32 [3072, 768], P('mp', 'dp'), may hold values from -0.21875 to 0.21875
- b_down: float32 [768], P(('dp', 'mp')), may hold values from -1.75 to 1.75
- ln2_gain: float32 [768], P(('dp', 'mp')), may hold values from 0.1 to 1.9
- ln2_bias: float32 [768], P(('dp', 'mp')), may hold values from -1.75 to 1.75
- cotangent: bfloat16 [16384, 768], P(('dp', 'mp')), may hold values from -6 to 6
Outputs:
- result: bfloat16 [16384, 768], P(('dp', 'mp'))
- grad_in: bfloat16 [16384, 768], P(('dp', 'mp'))
- grad_w_qkv: float32 [3, 768, 768], P(None, 'dp', 'mp')
- grad_b_qv: float32 [2, 768], P(None, ('dp', 'mp'))
- grad_w_out: float32 [768, 768], P('mp', 'dp')
- grad_b_out: float32 [768], P(('dp', 'mp'))
- grad_ln1_gain: float32 [768], P(('dp', 'mp'))
- grad_ln1_bias: float32 [768], P(('dp', 'mp'))
- grad_w_gu: float32 [2, 768, 3072], P(None, 'dp', 'mp')
- grad_b_gu: float32 [2, 3072], P(None, ('dp', 'mp'))
- grad_w_down: float32 [3072, 768], P('mp', 'dp')
- grad_b_down: float32 [768], P(('dp', 'mp'))
- grad_ln2_gain: float32 [768], P(('dp', 'mp'))
- grad_ln2_bias: float32 [768], P(('dp', 'mp'))
Inputs may be any that keep to these rules, and one draw needn't show every extreme that they name: `lengths`: the first sequence of every group has 1664 tokens; each row sums to 2048.
All inputs are finite; a program needn't handle non-finite values.
Results may differ from a plain program's by a relative error of at most 0.025.
Values may be sent and summed in bfloat16 or wider, within the bound.
A program may use at most 128 MiB of HBM per device.

v0:
```python
import jax
import jax.numpy as jnp
from jax import lax
from jax.sharding import PartitionSpec as P

HEAD = 64


def layer_norm(row_part, gain, shift):
    centre = row_part - jnp.mean(row_part, axis=-1, keepdims=True)
    spread = jnp.mean(centre * centre, axis=-1, keepdims=True)
    return centre * lax.rsqrt(spread + 1e-05) * gain + shift


def gated_unit(gate_pair):
    return jax.nn.gelu(gate_pair[:, 0], approximate=True) * gate_pair[:, 1]


def head_slopes(first_head, head_count):
    number = first_head + jnp.arange(head_count, dtype=jnp.int32)
    exponent = jnp.where(
        number < 8, number.astype(jnp.float32) + 1.0, number.astype(jnp.float32) - 7.5
    )
    return jnp.exp2(-exponent)


def segment_ids(seq_lengths, group_rows):
    seq_ends = jnp.cumsum(seq_lengths)
    places = jnp.arange(group_rows, dtype=jnp.int32)
    return jnp.sum((places[:, None] >= seq_ends[None, :]).astype(jnp.int32), axis=1)


def block_scores(q_part, key_rows, first_row, segment, slopes, score_scale):
    block_rows = q_part.shape[0]
    group_rows = key_rows.shape[0]
    raw_scores = jnp.einsum("bhe,khe->hbk", q_part, key_rows, preferred_element_type=jnp.float32)
    row_ids = first_row + jnp.arange(block_rows, dtype=jnp.int32)
    places = jnp.arange(group_rows, dtype=jnp.int32)
    distance = jnp.abs(row_ids[:, None] - places[None, :]).astype(jnp.float32)
    scaled = raw_scores * score_scale - slopes[:, None, None] * distance[None]
    same_seq = (
        lax.dynamic_slice_in_dim(segment, first_row, block_rows, 0)[:, None] == segment[None, :]
    )
    return jnp.where(same_seq[None], scaled, -1e30)


def per_device(
    hidden_in,
    lengths,
    w_qkv,
    b_qv,
    w_out,
    b_out,
    ln1_gain,
    ln1_bias,
    w_gu,
    b_gu,
    w_down,
    b_down,
    ln2_gain,
    ln2_bias,
    cotangent,
):
    mp_rank = lax.axis_index("mp")
    tok_dev = hidden_in.shape[0]
    group_rows = tok_dev * lax.axis_size("mp")
    block_rows = min(512, group_rows)
    starts = jnp.arange(group_rows // block_rows, dtype=jnp.int32) * block_rows
    score_scale = HEAD ** (-0.5)
    gathered_small = (
        lax.all_gather(b_qv, ("dp", "mp"), axis=1, tiled=True),
        lax.all_gather(b_out, ("dp", "mp"), axis=0, tiled=True),
        lax.all_gather(ln1_gain, ("dp", "mp"), axis=0, tiled=True),
        lax.all_gather(ln1_bias, ("dp", "mp"), axis=0, tiled=True),
        lax.all_gather(b_gu, ("dp", "mp"), axis=1, tiled=True),
        lax.all_gather(b_down, ("dp", "mp"), axis=0, tiled=True),
        lax.all_gather(ln2_gain, ("dp", "mp"), axis=0, tiled=True),
        lax.all_gather(ln2_bias, ("dp", "mp"), axis=0, tiled=True),
    )
    bias_qv, bias_out, gain_one, shift_one, bias_gu, bias_down, gain_two, shift_two = gathered_small
    qkv_mat, out_mat, gu_mat, down_mat = (
        lax.all_gather(w_qkv.astype(jnp.bfloat16), "dp", axis=1, tiled=True),
        lax.all_gather(w_out.astype(jnp.bfloat16), "dp", axis=1, tiled=True),
        lax.all_gather(w_gu.astype(jnp.bfloat16), "dp", axis=1, tiled=True),
        lax.all_gather(w_down.astype(jnp.bfloat16), "dp", axis=1, tiled=True),
    )
    head_cols = qkv_mat.shape[2]
    heads_dev = head_cols // HEAD
    ff_cols = gu_mat.shape[2]
    segment = segment_ids(lengths[0], group_rows)
    slopes = head_slopes(mp_rank * heads_dev, heads_dev)
    tokens = lax.all_gather(hidden_in, "mp", axis=0, tiled=True)
    qv_cols = lax.dynamic_slice_in_dim(bias_qv, mp_rank * head_cols, head_cols, 1)
    qkv_bias = jnp.stack([qv_cols[0], jnp.zeros_like(qv_cols[0]), qv_cols[1]])
    proj_qkv = (
        jnp.einsum("td,sdc->stc", tokens, qkv_mat, preferred_element_type=jnp.float32)
        + qkv_bias[:, None, :]
    ).astype(jnp.bfloat16)
    queries = proj_qkv[0].reshape(group_rows, heads_dev, HEAD)
    key_rows = proj_qkv[1].reshape(group_rows, heads_dev, HEAD)
    value_rows = proj_qkv[2].reshape(group_rows, heads_dev, HEAD)

    def one_block(first_row):
        q_part = lax.dynamic_slice_in_dim(queries, first_row, block_rows, 0)
        scaled = block_scores(q_part, key_rows, first_row, segment, slopes, score_scale)
        row_max = jnp.max(scaled, axis=-1, keepdims=True)
        exp_scores = jnp.exp(scaled - row_max)
        row_total = jnp.sum(exp_scores, axis=-1, keepdims=True)
        prob_rows = (exp_scores / row_total).astype(jnp.bfloat16)
        attn_part = jnp.einsum(
            "hbk,khe->bhe", prob_rows, value_rows, preferred_element_type=jnp.float32
        )
        return (attn_part, (row_max + jnp.log(row_total))[..., 0])

    attn_blocks, log_totals = lax.map(one_block, starts)
    attn_low = attn_blocks.reshape(group_rows, head_cols).astype(jnp.bfloat16)
    branch_attn = (
        lax.psum_scatter(
            jnp.dot(attn_low, out_mat, preferred_element_type=jnp.float32).astype(jnp.bfloat16),
            "mp",
            scatter_dimension=0,
            tiled=True,
        ).astype(jnp.float32)
        + bias_out
    )
    mid_rows, pull_one = jax.vjp(
        layer_norm, hidden_in.astype(jnp.float32) + branch_attn, gain_one, shift_one
    )
    mid_all = lax.all_gather(mid_rows.astype(jnp.bfloat16), "mp", axis=0, tiled=True)
    gu_cols = lax.dynamic_slice_in_dim(bias_gu, mp_rank * ff_cols, ff_cols, 1)
    gate_up = (
        jnp.einsum("td,sdf->tsf", mid_all, gu_mat, preferred_element_type=jnp.float32)
        + gu_cols[None]
    )
    act_rows, pull_glu = jax.vjp(gated_unit, gate_up)
    act_low = act_rows.astype(jnp.bfloat16)
    branch_ffn = (
        lax.psum_scatter(
            jnp.dot(act_low, down_mat, preferred_element_type=jnp.float32).astype(jnp.bfloat16),
            "mp",
            scatter_dimension=0,
            tiled=True,
        ).astype(jnp.float32)
        + bias_down
    )
    final_rows, pull_two = jax.vjp(layer_norm, mid_rows + branch_ffn, gain_two, shift_two)
    result = final_rows.astype(jnp.bfloat16)
    d_two, grad_gain_two, grad_shift_two = pull_two(cotangent.astype(jnp.float32))
    d_ffn = d_two.astype(jnp.bfloat16)
    grad_bias_down = jnp.sum(d_ffn.astype(jnp.float32), axis=0)
    d_ffn_all = lax.all_gather(d_ffn, "mp", axis=0, tiled=True)
    grad_down = jnp.einsum("tf,td->fd", act_low, d_ffn_all, preferred_element_type=jnp.float32)
    d_act = jnp.einsum("td,fd->tf", d_ffn_all, down_mat, preferred_element_type=jnp.float32)
    d_gate_up = pull_glu(d_act)[0].astype(jnp.bfloat16)
    gu_sums = jnp.sum(d_gate_up.astype(jnp.float32), axis=0)
    grad_bias_gu = lax.dynamic_update_slice_in_dim(
        jnp.zeros(bias_gu.shape, jnp.float32), gu_sums, mp_rank * ff_cols, 1
    )
    grad_gu = jnp.einsum("td,tsf->sdf", mid_all, d_gate_up, preferred_element_type=jnp.float32)
    d_mid = d_two + lax.psum_scatter(
        jnp.einsum("tsf,sdf->td", d_gate_up, gu_mat, preferred_element_type=jnp.float32).astype(
            jnp.bfloat16
        ),
        "mp",
        scatter_dimension=0,
        tiled=True,
    ).astype(jnp.float32)
    d_one, grad_gain_one, grad_shift_one = pull_one(d_mid)
    d_branch = d_one.astype(jnp.bfloat16)
    grad_bias_out = jnp.sum(d_branch.astype(jnp.float32), axis=0)
    d_branch_all = lax.all_gather(d_branch, "mp", axis=0, tiled=True)
    grad_out_mat = jnp.einsum(
        "tc,td->cd", attn_low, d_branch_all, preferred_element_type=jnp.float32
    )
    d_attn = (
        jnp.einsum("td,cd->tc", d_branch_all, out_mat, preferred_element_type=jnp.float32)
        .astype(jnp.bfloat16)
        .reshape(group_rows, heads_dev, HEAD)
    )

    def back_block(carried, block_item):
        grad_keys, grad_vals = carried
        first_row, lse_rows = block_item
        q_part = lax.dynamic_slice_in_dim(queries, first_row, block_rows, 0)
        g_part = lax.dynamic_slice_in_dim(d_attn, first_row, block_rows, 0)
        scaled = block_scores(q_part, key_rows, first_row, segment, slopes, score_scale)
        prob_rows = jnp.exp(scaled - lse_rows[..., None])
        grad_vals = grad_vals + jnp.einsum(
            "hbk,bhe->khe",
            prob_rows.astype(jnp.bfloat16),
            g_part,
            preferred_element_type=jnp.float32,
        )
        d_prob = jnp.einsum("bhe,khe->hbk", g_part, value_rows, preferred_element_type=jnp.float32)
        inner = jnp.sum(prob_rows * d_prob, axis=-1, keepdims=True)
        d_raw = (score_scale * prob_rows * (d_prob - inner)).astype(jnp.bfloat16)
        d_query = jnp.einsum("hbk,khe->bhe", d_raw, key_rows, preferred_element_type=jnp.float32)
        grad_keys = grad_keys + jnp.einsum(
            "hbk,bhe->khe", d_raw, q_part, preferred_element_type=jnp.float32
        )
        return ((grad_keys, grad_vals), d_query)

    zero_keys = jnp.zeros(key_rows.shape, jnp.float32)
    (grad_keys, grad_vals), d_queries = lax.scan(
        back_block, (zero_keys, zero_keys), (starts, log_totals)
    )
    d_qkv = jnp.stack(
        [
            d_queries.reshape(group_rows, head_cols),
            grad_keys.reshape(group_rows, head_cols),
            grad_vals.reshape(group_rows, head_cols),
        ]
    ).astype(jnp.bfloat16)
    column_sums = jnp.sum(d_qkv.astype(jnp.float32), axis=1)
    grad_bias_qv = lax.dynamic_update_slice_in_dim(
        jnp.zeros(bias_qv.shape, jnp.float32),
        jnp.stack([column_sums[0], column_sums[2]]),
        mp_rank * head_cols,
        1,
    )
    grad_qkv = jnp.einsum("td,stc->sdc", tokens, d_qkv, preferred_element_type=jnp.float32)
    grad_input = (
        d_one
        + lax.psum_scatter(
            jnp.einsum("stc,sdc->td", d_qkv, qkv_mat, preferred_element_type=jnp.float32).astype(
                jnp.bfloat16
            ),
            "mp",
            scatter_dimension=0,
            tiled=True,
        ).astype(jnp.float32)
    ).astype(jnp.bfloat16)
    small_shards = (
        lax.psum_scatter(grad_bias_qv, ("dp", "mp"), scatter_dimension=1, tiled=True),
        lax.psum_scatter(grad_bias_out, ("dp", "mp"), scatter_dimension=0, tiled=True),
        lax.psum_scatter(grad_gain_one, ("dp", "mp"), scatter_dimension=0, tiled=True),
        lax.psum_scatter(grad_shift_one, ("dp", "mp"), scatter_dimension=0, tiled=True),
        lax.psum_scatter(grad_bias_gu, ("dp", "mp"), scatter_dimension=1, tiled=True),
        lax.psum_scatter(grad_bias_down, ("dp", "mp"), scatter_dimension=0, tiled=True),
        lax.psum_scatter(grad_gain_two, ("dp", "mp"), scatter_dimension=0, tiled=True),
        lax.psum_scatter(grad_shift_two, ("dp", "mp"), scatter_dimension=0, tiled=True),
    )
    grad_qkv_shard, grad_out_shard, grad_gu_shard, grad_down_shard = (
        lax.psum_scatter(
            grad_qkv.astype(jnp.bfloat16), "dp", scatter_dimension=1, tiled=True
        ).astype(jnp.float32),
        lax.psum_scatter(
            grad_out_mat.astype(jnp.bfloat16), "dp", scatter_dimension=1, tiled=True
        ).astype(jnp.float32),
        lax.psum_scatter(
            grad_gu.astype(jnp.bfloat16), "dp", scatter_dimension=1, tiled=True
        ).astype(jnp.float32),
        lax.psum_scatter(
            grad_down.astype(jnp.bfloat16), "dp", scatter_dimension=1, tiled=True
        ).astype(jnp.float32),
    )
    return (
        result,
        grad_input,
        grad_qkv_shard,
        small_shards[0],
        grad_out_shard,
        small_shards[1],
        small_shards[2],
        small_shards[3],
        grad_gu_shard,
        small_shards[4],
        grad_down_shard,
        small_shards[5],
        small_shards[6],
        small_shards[7],
    )


def solution(mesh):
    in_specs = (
        P(("dp", "mp"), None),
        P("dp", None),
        P(None, "dp", "mp"),
        P(None, ("dp", "mp")),
        P("mp", "dp"),
        P(("dp", "mp")),
        P(("dp", "mp")),
        P(("dp", "mp")),
        P(None, "dp", "mp"),
        P(None, ("dp", "mp")),
        P("mp", "dp"),
        P(("dp", "mp")),
        P(("dp", "mp")),
        P(("dp", "mp")),
        P(("dp", "mp"), None),
    )
    out_specs = (
        P(("dp", "mp"), None),
        P(("dp", "mp"), None),
        P(None, "dp", "mp"),
        P(None, ("dp", "mp")),
        P("mp", "dp"),
        P(("dp", "mp")),
        P(("dp", "mp")),
        P(("dp", "mp")),
        P(None, "dp", "mp"),
        P(None, ("dp", "mp")),
        P("mp", "dp"),
        P(("dp", "mp")),
        P(("dp", "mp")),
        P(("dp", "mp")),
    )
    return jax.shard_map(
        per_device, mesh=mesh, in_specs=in_specs, out_specs=out_specs, check_vma=False
    )
```

profile of v0, /device:TPU:0, one launch (start us, length us, event | category | flops | bytes accessed | tf_op | source)
XLA Modules:
  0.0 991.9 jit_solution(9109078191257354017)
XLA Ops:
  9.6 71.1 %all-gather = f32[32,24,2]{1,2,0:T(2,128)S(1)} all-gather(f32[1,24,2]{1,2,0:T(2,128)} %bitcast.192), channel_id=1, replica_groups=mesh['dp'=8,'mp'=4] {'dp','mp'}, dimensions={0}, use_global_device_ids=true | all-gather | bytes 6336 | tf_op jit(solution)/shard_map/all_gather | solution.py:71
  83.0 9.6 all_gather.51
  93.3 13.4 %all_gather.48 = bf16[3,768,192]{2,0,1:T(4,128)(2,1)S(1)} all-gather(bf16[3,96,192]{2,0,1:T(4,128)(2,1)S(1)} %copy.68), channel_id=1, replica_groups=mesh['dp'=8,'mp'=4] {'dp'}, dimensions={1}, use_global_device_ids=true | all-gather | bytes 995328 | tf_op jit(solution)/shard_map/all_gather | solution.py:82
  107.9 4.7 fusion.51
  112.8 77.4 %while.28 = (s32[]{:T(128)}, bf16[4,512,3,64]{1,3,2,0:T(8,128)(2,1)S(1)}, f32[4,3,512]{2,1,0:T(4,128)}, s32[4]{0:T(128)}, s32[2048]{0:T(1024)S(1)}, /*index=5*/b...) while((s32[]{:T(128)}, ...), condition=%wide.region_5.6_spmd.clone, body=%wide.region_2.5_spmd.clone.sunk | while | flops 866122752 | bytes 60957912 | solution.py:115
  122.5 4.5 fusion.122
  127.0 4.7 fusion.123
  141.8 4.5 fusion.122
  146.3 4.7 fusion.123
  161.1 4.5 fusion.122
  165.6 4.7 fusion.123
  180.4 4.5 fusion.122
  184.9 4.7 fusion.123
  197.2 40.9 %all-reduce.17 = (f32[768]{0:T(1024)S(1)}, f32[768]{0:T(1024)}, f32[768]{0:T(1024)}, f32[768]{0:T(1024)}, f32[768]{0:T(1024)}) all-reduce(f32[768]{0:T(1024)S(1)} %dynamic-update-slice, f32[768]{0:T(1024)S(1)} %dynamic-update-slice.2, f32[768]{0:T(1024)S(1)} %dynamic-update-slice.1, ...), channel_id=1, replica_groups=mesh['dp'=8,'mp'=4] {'dp','mp'}, use_global_device_ids=true, to_apply=%add.2 | all-reduce | flops 3840 | bytes 30720
  238.1 15.5 %reduce-scatter.16.cloned.1.call-done = bf16[512,768]{1,0:T(8,128)(2,1)} async-done(((bf16[2048,768]{1,0:T(8,128)(2,1)}), bf16[512,768]{1,0:T(8,128)(2,1)}) %reduce-scatter.16.cloned.1.call-update) | async-done | bytes 786448 | tf_op jit(solution)/shard_map/reduce_scatter | solution.py:118
  261.0 68.3 %all-gather.1 = f32[32,96,2]{1,2,0:T(2,128)S(1)} all-gather(f32[1,96,2]{1,2,0:T(2,128)} %bitcast.193), channel_id=1, replica_groups=mesh['dp'=8,'mp'=4] {'dp','mp'}, dimensions={0}, use_global_device_ids=true | all-gather | bytes 25344 | tf_op jit(solution)/shard_map/all_gather | solution.py:75
  332.6 7.8 broadcast_add_fusion
  340.4 4.6 copy-done.13
  348.4 6.5 convolution_convert_fusion
  355.2 59.5 %reduce-scatter.18.cloned.1.call-done = bf16[512,768]{1,0:T(8,128)(2,1)} async-done(((bf16[2048,768]{1,0:T(8,128)(2,1)}), bf16[512,768]{1,0:T(8,128)(2,1)}) %reduce-scatter.18.cloned.1.call-update) | async-done | bytes 786448 | tf_op jit(solution)/shard_map/reduce_scatter | solution.py:138
  421.8 63.5 %all-gather.17.cloned.1.call-done = bf16[2048,768]{1,0:T(8,128)(2,1)} async-done(((bf16[512,768]{1,0:T(8,128)(2,1)}), bf16[2048,768]{1,0:T(8,128)(2,1)}) %all-gather.17.cloned.1.call-update) | async-done | bytes 3145744 | tf_op jit(solution)/shard_map/all_gather | solution.py:151
  485.4 10.7 %multiply_bitcast_fusion = (f32[2048,1,768]{2,0,1:T(8,128)S(1)}, f32[2048,1,768]{2,0,1:T(8,128)S(1)}) fusion(f32[2048,2,768]{2,0,1:T(8,128)} %copy-done.13, bf16[2048,768]{1,0:T(8,128)(2,1)} %all-gather.17.cloned.1.call-done, bf16[768,768]{0,1:T(8,128)(2,1)} %all-gather.15.cloned.1.call-done), kind=kOutput, calls=%fused_computation.64 | convolution fusion | flops 2450522112 | bytes 29491200 | tf_op jit(solution)/shard_map/td,fd->tf/dot_general | solution.py:153
  500.6 6.4 bitcast_convert_fusion.1
  507.1 59.0 %reduce-scatter.20.cloned.1.call-done = bf16[512,768]{1,0:T(8,128)(2,1)} async-done(((bf16[2048,768]{1,0:T(8,128)(2,1)}), bf16[512,768]{1,0:T(8,128)(2,1)}) %reduce-scatter.20.cloned.1.call-update) | async-done | bytes 786448 | tf_op jit(solution)/shard_map/reduce_scatter | solution.py:160
  575.0 5.3 convert_reduce_fusion
  582.0 10.6 %convert_bitcast_fusion = bf16[2,768,768]{1,2,0:T(8,128)(2,1)} fusion(bf16[2048,768]{1,0:T(8,128)(2,1)} %all-gather.11.cloned.1.call-done, f32[2048,1,768]{2,0,1:T(8,128)} %copy-done.18, f32[2048,1,768]{2,0,1:T(8,128)} %copy-done.17), kind=kOutput, calls=%fused_computation.87 | convolution fusion | flops 4839309312 | bytes 18087936 | tf_op jit(solution)/shard_map/td,tsf->sdf/dot_general | solution.py:159
  592.6 6.9 copy.77
  599.6 6.5 convolution_convert_fusion.3
  606.6 31.8 %all-gather.19.cloned.1.call-done = bf16[2048,768]{1,0:T(8,128)(2,1)} async-done(((bf16[512,768]{1,0:T(8,128)(2,1)}), bf16[2048,768]{1,0:T(8,128)(2,1)}) %all-gather.19.cloned.1.call-update) | async-done | bytes 3145744 | tf_op jit(solution)/shard_map/all_gather | solution.py:171
  643.3 152.4 %while.29 = (s32[]{:T(128)}, f32[2048,3,64]{0,2,1:T(8,128)}, f32[2048,3,64]{0,2,1:T(8,128)}, bf16[4,512,3,64]{1,3,2,0:T(8,128)(2,1)}, s32[4]{0:T(128)}, /*index=...) while((s32[]{:T(128)}, f32[2048,3,64]{0,2,1:T(8,128)}, ...), condition=%wide.region_19.20_spmd.clone, body=%wide.region_17.19_spmd.clone.sunk | while | flops 2056780800 | bytes 146195408 | solution.py:204
  652.8 10.1 %multiply_reduce_fusion.6 = (f32[3,512]{1,0:T(4,128)S(1)}, f32[3,512,2048]{2,1,0:T(8,128)}) fusion(f32[3,512,2048]{2,1,0:T(8,128)S(1)} %fusion.133, f32[3,512]{1,0:T(4,128)S(1)} %dynamic-slice_bitcast_fusion.4, f32[512,2048]{1,0:T(8,128)S(1)} %abs_convert_fusion.5, f32[3]{0:T(128)} %multiply_exponential_fusion.5, ...), kind=kOutput, calls=%fused_computation.23.clone.1 | convolution fusion | flops 424671744 | bytes 31404548 | tf_op jit(solution)/shard_map/while/body/eval_jaxpr/bhe,khe->hbk/dot_general | solution.py:36
  662.9 6.1 multiply_convert_fusion.3
  669.0 6.4 fusion.135
  690.9 10.1 %multiply_reduce_fusion.6 = (f32[3,512]{1,0:T(4,128)S(1)}, f32[3,512,2048]{2,1,0:T(8,128)}) fusion(f32[3,512,2048]{2,1,0:T(8,128)S(1)} %fusion.133, f32[3,512]{1,0:T(4,128)S(1)} %dynamic-slice_bitcast_fusion.4, f32[512,2048]{1,0:T(8,128)S(1)} %abs_convert_fusion.5, f32[3]{0:T(128)} %multiply_exponential_fusion.5, ...), kind=kOutput, calls=%fused_computation.23.clone.1 | convolution fusion | flops 424671744 | bytes 31404548 | tf_op jit(solution)/shard_map/while/body/eval_jaxpr/bhe,khe->hbk/dot_general | solution.py:36
  701.0 6.0 multiply_convert_fusion.3
  707.0 6.4 fusion.135
  728.8 10.1 %multiply_reduce_fusion.6 = (f32[3,512]{1,0:T(4,128)S(1)}, f32[3,512,2048]{2,1,0:T(8,128)}) fusion(f32[3,512,2048]{2,1,0:T(8,128)S(1)} %fusion.133, f32[3,512]{1,0:T(4,128)S(1)} %dynamic-slice_bitcast_fusion.4, f32[512,2048]{1,0:T(8,128)S(1)} %abs_convert_fusion.5, f32[3]{0:T(128)} %multiply_exponential_fusion.5, ...), kind=kOutput, calls=%fused_computation.23.clone.1 | convolution fusion | flops 424671744 | bytes 31404548 | tf_op jit(solution)/shard_map/while/body/eval_jaxpr/bhe,khe->hbk/dot_general | solution.py:36
  738.9 5.9 multiply_convert_fusion.3
  744.9 6.8 fusion.135
  767.1 10.1 %multiply_reduce_fusion.6 = (f32[3,512]{1,0:T(4,128)S(1)}, f32[3,512,2048]{2,1,0:T(8,128)}) fusion(f32[3,512,2048]{2,1,0:T(8,128)S(1)} %fusion.133, f32[3,512]{1,0:T(4,128)S(1)} %dynamic-slice_bitcast_fusion.4, f32[512,2048]{1,0:T(8,128)S(1)} %abs_convert_fusion.5, f32[3]{0:T(128)} %multiply_exponential_fusion.5, ...), kind=kOutput, calls=%fused_computation.23.clone.1 | convolution fusion | flops 424671744 | bytes 31404548 | tf_op jit(solution)/shard_map/while/body/eval_jaxpr/bhe,khe->hbk/dot_general | solution.py:36
  777.2 6.1 multiply_convert_fusion.3
  783.4 6.3 fusion.135
  805.6 4.8 fusion.65
  815.3 6.1 bitcast_convert_fusion
  827.1 16.7 %reduce-scatter.24.cloned.1.call-done = bf16[768,96]{0,1:T(8,128)(2,1)} async-done(((bf16[768,768]{0,1:T(8,128)(2,1)}), bf16[768,96]{0,1:T(8,128)(2,1)}) %reduce-scatter.24.cloned.1.call-update) | async-done | bytes 147472 | tf_op jit(solution)/shard_map/reduce_scatter | solution.py:253
  847.8 40.1 %all-reduce.16 = (f32[768]{0:T(1024)S(1)}, f32[2,768]{1,0:T(2,128)S(1)}, f32[768]{0:T(1024)S(1)}, f32[768]{0:T(1024)S(1)}, f32[768]{0:T(1024)S(1)}, /*index=5*/f...) all-reduce(f32[768]{0:T(1024)S(1)} %dynamic-update-slice.5, ...), channel_id=1, replica_groups=mesh['dp'=8,'mp'=4] {'dp','mp'}, use_global_device_ids=true, to_apply=%add.7 | all-reduce | flops 6912 | bytes 55296
  894.8 24.7 %reduce-scatter.26.cloned.1.call-done = bf16[96,576]{1,0:T(8,128)(2,1)} async-done(((bf16[768,576]{1,0:T(8,128)(2,1)}), bf16[96,576]{1,0:T(8,128)(2,1)}) %reduce-scatter.26.cloned.1.call-update) | async-done | bytes 110608
  921.7 60.5 %reduce-scatter.22.cloned.1.call-done = bf16[512,768]{1,0:T(8,128)(2,1)} async-done(((bf16[2048,768]{1,0:T(8,128)(2,1)}), bf16[512,768]{1,0:T(8,128)(2,1)}) %reduce-scatter.22.cloned.1.call-update) | async-done | bytes 786448 | tf_op jit(solution)/shard_map/reduce_scatter | solution.py:224
  (352 shorter events, 175.4 us)
Async XLA Ops:
  8.0 98.8 %all-gather.9.cloned.1.call-start = ((), (), s32[]{:S(2)}) async-start(), calls=%async_computation.8 | async-start | bytes 3932160 | tf_op jit(solution)/shard_map/all_gather | solution.py:92
  8.7 244.8 %reduce-scatter.16.cloned.1.call-start = ((), (), s32[]{:S(2)}) async-start(), calls=%async_computation.9 | async-start | bytes 3932160 | tf_op jit(solution)/shard_map/reduce_scatter | solution.py:118
  194.7 58.9 %copy-start.7 = (bf16[512,768]{1,0:T(8,128)(2,1)S(1)}, bf16[512,768]{1,0:T(8,128)(2,1)}, u32[]{:S(2)}) copy-start(bf16[512,768]{1,0:T(8,128)(2,1)} %param.19) | copy-start | bytes 2359300
  194.7 137.9 %all-gather.13.cloned.1.call-start = ((), (), s32[]{:S(2)}) async-start(), calls=%async_computation.11 | async-start | bytes 2654208 | tf_op jit(solution)/shard_map/all_gather | solution.py:84
  195.6 137.1 %all-gather.11.cloned.1.call-start = ((), (), s32[]{:S(2)}) async-start(), calls=%async_computation.10 | async-start | bytes 3932160 | tf_op jit(solution)/shard_map/all_gather | solution.py:129
  253.6 4.3 copy-start.8
  253.6 4.3 copy-start.29
  253.6 4.3 copy-start.46
  259.2 89.2 %all-gather.15.cloned.1.call-start = ((), (), s32[]{:S(2)}) async-start(), calls=%async_computation.12 | async-start | bytes 1327104 | tf_op jit(solution)/shard_map/all_gather | solution.py:85
  260.9 153.8 %reduce-scatter.18.cloned.1.call-start = ((), (), s32[]{:S(2)}) async-start(), calls=%async_computation.13 | async-start | bytes 3932160 | tf_op jit(solution)/shard_map/reduce_scatter | solution.py:138
  340.4 4.6 copy-start.13
  355.0 130.4 %all-gather.17.cloned.1.call-start = ((), (), s32[]{:S(2)}) async-start(), calls=%async_computation.14 | async-start | bytes 3932160 | tf_op jit(solution)/shard_map/all_gather | solution.py:151
  421.8 144.4 %reduce-scatter.20.cloned.1.call-start = ((), (), s32[]{:S(2)}) async-start(), calls=%async_computation.15 | async-start | bytes 3932160 | tf_op jit(solution)/shard_map/reduce_scatter | solution.py:160
  485.4 15.3 %copy-start.49 = (bf16[2,768,768]{2,1,0:T(8,128)(2,1)S(1)}, bf16[2,768,768]{2,1,0:T(8,128)(2,1)}, u32[]{:S(2)}) copy-start(bf16[2,768,768]{2,1,0:T(8,128)(2,1)} %all-gather.13.cloned.1.call-done) | copy-start | bytes 7077892
  496.1 4.6 copy-start.18
  507.1 131.3 %all-gather.19.cloned.1.call-start = ((), (), s32[]{:S(2)}) async-start(), calls=%async_computation.16 | async-start | bytes 3932160 | tf_op jit(solution)/shard_map/all_gather | solution.py:171
  566.1 4.1 copy-start.10
  566.1 4.1 copy-start.26
  566.1 4.1 copy-start.30
  574.9 248.7 %reduce-scatter.30.cloned.1.call-start = ((), (), s32[]{:S(2)}) async-start(), calls=%async_computation.21 | async-start | bytes 1622016
  582.0 243.1 %all-reduce.20.cloned.1.call-start = ((), (), s32[]{:S(2)}) async-start(), calls=%async_computation.22 | async-start | bytes 4718592
  599.5 244.3 %reduce-scatter.24.cloned.1.call-start = ((), (), s32[]{:S(2)}) async-start(), calls=%async_computation.18 | async-start | bytes 1327104 | tf_op jit(solution)/shard_map/reduce_scatter | solution.py:253
  606.1 287.2 %reduce-scatter.28.cloned.1.call-start = ((), (), s32[]{:S(2)}) async-start(), calls=%async_computation.20 | async-start | bytes 442368
  662.9 6.1 copy-start.3
  669.0 6.5 copy-start.20
  701.0 6.0 copy-start.3
  707.0 6.4 copy-start.20
  738.9 6.0 copy-start.3
  744.9 6.8 copy-start.20
  777.2 6.2 copy-start.3
  783.4 6.3 copy-start.20
  797.6 5.2 copy-start.2
  801.8 3.8 copy-start.22
  802.9 12.4 %copy-start.24 = (bf16[2048,3,64]{0,2,1:T(8,128)(2,1)}, bf16[2048,3,64]{0,2,1:T(8,128)(2,1)S(1)}, u32[]{:S(2)}) copy-start(bf16[2048,3,64]{0,2,1:T(8,128)(2,1)S(1)} %convert.13) | copy-start | bytes 2359300
  804.7 114.8 %reduce-scatter.26.cloned.1.call-start = ((), (), s32[]{:S(2)}) async-start(), calls=%async_computation.19 | async-start | bytes 1105920
  815.3 166.9 %reduce-scatter.22.cloned.1.call-start = ((), (), s32[]{:S(2)}) async-start(), calls=%async_computation.17 | async-start | bytes 3932160 | tf_op jit(solution)/shard_map/reduce_scatter | solution.py:224
  821.5 26.3 %copy-start.42 = (f32[768]{0:T(1024)S(1)}, f32[768]{0:T(1024)}, u32[]{:S(2)}) copy-start(f32[768]{0:T(1024)} %get-tuple-element.266) | copy-start | bytes 9220
  821.5 26.3 %copy-start.43 = (f32[768]{0:T(1024)S(1)}, f32[768]{0:T(1024)}, u32[]{:S(2)}) copy-start(f32[768]{0:T(1024)} %get-tuple-element.269) | copy-start | bytes 9220
  821.5 26.3 %copy-start.44 = (f32[768]{0:T(1024)S(1)}, f32[768]{0:T(1024)}, u32[]{:S(2)}) copy-start(f32[768]{0:T(1024)} %get-tuple-element.325) | copy-start | bytes 9220
  821.5 26.3 %copy-start.45 = (f32[768]{0:T(1024)S(1)}, f32[768]{0:T(1024)}, u32[]{:S(2)}) copy-start(f32[768]{0:T(1024)} %get-tuple-element.327) | copy-start | bytes 9220
  821.5 26.3 %copy-start.47 = (f32[768]{0:T(1024)S(1)}, f32[768]{0:T(1024)}, u32[]{:S(2)}) copy-start(f32[768]{0:T(1024)} %get-tuple-element.264) | copy-start | bytes 9220
  821.5 26.3 %copy-start.48 = (f32[768]{0:T(1024)S(1)}, f32[768]{0:T(1024)}, u32[]{:S(2)}) copy-start(f32[768]{0:T(1024)} %get-tuple-element.268) | copy-start | bytes 9220
  821.5 70.5 %copy-start.6 = (f32[512,768]{1,0:T(8,128)S(1)}, f32[512,768]{1,0:T(8,128)}, u32[]{:S(2)}) copy-start(f32[512,768]{1,0:T(8,128)} %copy-done.5) | copy-start | bytes 4718596
  821.5 70.5 %copy-start.33 = (f32[512]{0:T(512)S(1)}, f32[512]{0:T(512)}, u32[]{:S(2)}) copy-start(f32[512]{0:T(512)} %copy-done.32) | copy-start | bytes 6148
  821.6 70.5 %copy-start.35 = (f32[768]{0:T(1024)S(1)}, f32[768]{0:T(1024)}, u32[]{:S(2)}) copy-start(f32[768]{0:T(1024)} %get-tuple-element.324) | copy-start | bytes 9220
  821.6 70.5 %copy-start.38 = (f32[512]{0:T(512)S(1)}, f32[512]{0:T(512)}, u32[]{:S(2)}) copy-start(f32[512]{0:T(512)} %copy-done.37) | copy-start | bytes 6148
  845.4 136.7 %copy-start.12 = (f32[512,768]{1,0:T(8,128)S(1)}, f32[512,768]{1,0:T(8,128)}, u32[]{:S(2)}) copy-start(f32[512,768]{1,0:T(8,128)} %copy-done.11) | copy-start | bytes 4718596
  845.4 136.7 %copy-start.41 = (f32[512]{0:T(512)S(1)}, f32[512]{0:T(512)}, u32[]{:S(2)}) copy-start(f32[512]{0:T(512)} %copy-done.40) | copy-start | bytes 6148
  (42 other events, 78.0 us)
Sparse Core Ops, SparseCore 0:
  10.4 66.3 all-gather.8
  194.9 58.6 reduce-scatter.15
  421.9 63.4 all-gather.16
  507.2 58.8 reduce-scatter.19
Sparse Core Ops, SparseCore 1:
  197.7 26.2 all-gather.12
  259.3 63.5 all-gather.10
  325.2 22.6 all-gather.14
  355.1 59.6 reduce-scatter.17
  575.0 63.3 all-gather.18
  643.7 95.7 reduce-scatter.29
  742.6 61.5 all-reduce.19
  807.6 36.1 reduce-scatter.23
  846.7 33.8 reduce-scatter.27
  883.9 35.6 reduce-scatter.25
  921.8 60.2 reduce-scatter.21
where the time goes:
time: 998 us; the launch traced here: 992 us
  waiting for transfers between devices  332 us (33%)
  blocking collectives  243 us (24%)
  matrix products  206 us (21%)
  other arithmetic  105 us (11%)
  local copies, waits for them, and re-layouts  70.4 us (7%)
  between operations  17.1 us (2%)
  loops' own time  16.6 us (2%)
    unnamed x2, blocking collectives  81 us
    all_gather x1, blocking collectives, per_device(): lax.all_gather(b_qv, ('dp', 'mp'), axis=1, tiled=True)  71.1 us
    all_gather x1, blocking collectives, per_device(): lax.all_gather(b_gu, ('dp', 'mp'), axis=1, tiled=True)  68.3 us
    all_gather x1, waiting for transfers between devices, per_device(): d_ffn_all = lax.all_gather(d_ffn, 'mp', axis=0, tiled=True)  63.5 us
    reduce_scatter x1, waiting for transfers between devices, per_device(): lax.psum_scatter(jnp.einsum('stc,sdc->td', d_qkv, qkv_mat, preferred_elem...  60.5 us
    reduce_scatter x1, waiting for transfers between devices, per_device(): lax.psum_scatter(jnp.dot(act_low, down_mat, preferred_element_type=jnp.fl...  59.5 us
    reduce_scatter x1, waiting for transfers between devices, per_device(): lax.psum_scatter(jnp.einsum('tsf,sdf->td', d_gate_up, gu_mat, preferred_e...  59 us
    dot_general x8, matrix products, block_scores(): jnp.einsum('bhe,khe->hbk', q_part, key_rows, preferred_element_type=jnp.f...  57 us
  transfers between devices with their start and end apart: 15, of which 8 were waited for; matrix products, arithmetic and copies ran while one was open for 25% of the time, Pallas kernels for 0%

commit v1 on v0

v1 whole, which is shorter than its diff:
```python
import functools

import jax
import jax.numpy as jnp
from jax import lax
from jax.experimental import pallas as pl
from jax.experimental.pallas import tpu as pltpu
from jax.sharding import PartitionSpec as P

HEAD = 64
LONGEST = 1664
QB = 256
BF = jnp.bfloat16
F32 = jnp.float32
VMEM_LIMIT = 56 * 1024 * 1024


def dot(a, b):
    return lax.dot_general(a, b, (((1,), (0,)), ((), ())), preferred_element_type=F32)


def dot_nt(a, b):
    return lax.dot_general(a, b, (((1,), (1,)), ((), ())), preferred_element_type=F32)


def vmem():
    return pl.BlockSpec(memory_space=pltpu.VMEM)


def smem():
    return pl.BlockSpec(memory_space=pltpu.SMEM)


def hbm():
    return pl.BlockSpec(memory_space=pl.ANY)


def query_blocks(longest):
    whole = longest // QB
    rest = longest - whole * QB
    return whole, rest


def attention_forward(
    x, w, bias, slope, length, qkv, o, u, p, p2, kt, vext, dist, pbuf, psem
):
    group = x.shape[0]
    own = o.shape[1]
    cols = w.shape[2]
    heads = cols // HEAD
    tail = group - LONGEST
    for c in range(0, group, own):
        rows = pl.ds(c, own)
        xc = x[rows, :]
        q = (dot(xc, w[0]) + bias[0:1, :]).astype(BF)
        qkv[0, rows, :] = q * jnp.asarray(HEAD**-0.5, BF)
        k = (dot(xc, w[1]) + bias[1:2, :]).astype(BF)
        qkv[1, rows, :] = k
        kt[:, rows] = k.astype(F32).T.astype(BF)
        v = (dot(xc, w[2]) + bias[2:3, :]).astype(BF)
        qkv[2, rows, :] = v
        one = jnp.where(lax.broadcasted_iota(jnp.int32, (own, HEAD), 1) == 0, 1.0, 0.0)
        for h in range(heads):
            vh = v[:, h * HEAD : (h + 1) * HEAD].astype(F32)
            vext[h, rows, :] = jnp.concatenate([vh, one], axis=1).astype(BF)
    width = dist.shape[1]
    base = width - LONGEST
    i = lax.broadcasted_iota(jnp.int32, (QB, width), 0)
    j = lax.broadcasted_iota(jnp.int32, (QB, width), 1)
    dist[...] = jnp.abs(i + base - j).astype(F32)

    def softmax_block(s):
        m = jnp.max(s, axis=1, keepdims=True)
        return jnp.exp(s - m).astype(BF)

    def finish(h, row, rows, uu):
        u[h, pl.ds(row, rows), :] = uu
        return (uu[:, :HEAD] * (1.0 / uu[:, HEAD : HEAD + 1])).astype(BF)

    whole, rest = query_blocks(LONGEST)
    for h in range(heads):
        hs = slice(h * HEAD, (h + 1) * HEAD)
        sl = slope[h]

        def long_block(row, rows, slot):
            qh = qkv[0, pl.ds(row, rows), hs]
            s = dot(qh, kt[hs, :LONGEST])
            off = pl.multiple_of(base - row, 128)
            s = s - sl * dist[:rows, pl.ds(off, LONGEST)]
            pb = softmax_block(s)
            pbuf[slot, :rows, :] = pb
            uu = dot(pb, vext[h, :LONGEST, :])
            return finish(h, row, rows, uu)

        def copy_out(row, rows, slot):
            return pltpu.make_async_copy(
                pbuf.at[slot, pl.ds(0, rows), :],
                p.at[h, pl.ds(row, rows), :],
                psem.at[slot],
            )

        def step(b, _):
            row = pl.multiple_of(b * QB, QB)
            slot = lax.rem(b, 2)

            @pl.when(b >= 2)
            def _():
                copy_out(row - 2 * QB, QB, slot).wait()

            oh = long_block(row, QB, slot)
            copy_out(row, QB, slot).start()
            o[row // own, pl.ds(pl.multiple_of(row % own, QB), QB), hs] = oh
            return 0

        lax.fori_loop(0, whole, step, 0)
        copy_out((whole - 2) * QB, QB, whole % 2).wait()
        row = whole * QB
        oh = long_block(row, rest, whole % 2)
        copy_out(row, rest, whole % 2).start()
        o[row // own, pl.ds(row % own, rest), hs] = oh
        copy_out((whole - 1) * QB, QB, (whole - 1) % 2).wait()
        qh = qkv[0, LONGEST:, hs]
        s = dot(qh, kt[hs, LONGEST:])
        ii = lax.broadcasted_iota(jnp.int32, (tail, tail), 0)
        jj = lax.broadcasted_iota(jnp.int32, (tail, tail), 1)
        s = s - sl * jnp.abs(ii - jj).astype(F32)
        cut = length[0, 1]
        same = (ii < cut) == (jj < cut)
        s = jnp.where(same, s, -1e30)
        pb = softmax_block(s)
        p2[h] = pb
        uu = dot(pb, vext[h, LONGEST:, :])
        oh = finish(h, LONGEST, tail, uu)
        o[LONGEST // own, pl.ds(LONGEST % own, tail), hs] = oh
        copy_out(row, rest, whole % 2).wait()


def attention_backward(qkv, g, u, p, p2, d, vt, pbuf, dkt, dvt, psem):
    group = qkv.shape[1]
    own = d.shape[2]
    cols = qkv.shape[2]
    heads = cols // HEAD
    tail = group - LONGEST
    whole, rest = query_blocks(LONGEST)
    for c in range(0, group, own):
        rows = pl.ds(c, own)
        v = qkv[2, rows, :]
        vtc = v.astype(F32).T
        extra = jnp.where(lax.broadcasted_iota(jnp.int32, (HEAD, own), 0) < 2, -1.0, 0.0)
        for h in range(heads):
            vt[h, :, rows] = jnp.concatenate(
                [vtc[h * HEAD : (h + 1) * HEAD], extra], axis=0
            ).astype(BF)

    for h in range(heads):
        hs = slice(h * HEAD, (h + 1) * HEAD)

        def block(row, rows, chunk, place, pb, keys, first):
            uu = u[h, pl.ds(row, rows), :]
            inv = 1.0 / uu[:, HEAD : HEAD + 1]
            gg = g[chunk, pl.ds(place, rows), hs].astype(F32) * inv
            total = jnp.sum(gg * uu[:, :HEAD], axis=1, keepdims=True) * inv
            high = total.astype(BF).astype(F32)
            low = total - high
            lane = lax.broadcasted_iota(jnp.int32, (rows, HEAD), 1)
            extra = jnp.where(lane == 0, high, jnp.where(lane == 1, low, 0.0))
            gext = jnp.concatenate([gg, extra], axis=1).astype(BF)
            dp = dot(gext, vt[h, :, keys])
            ds = (pb.astype(F32) * dp).astype(BF)
            dq = dot(ds, qkv[1, keys, hs]) * (HEAD**-0.5)
            d[chunk, 0, pl.ds(place, rows), hs] = dq.astype(BF)
            qt = qkv[0, pl.ds(row, rows), hs].astype(F32).T.astype(BF)
            gt = gg.T.astype(BF)
            dk = dot(qt, ds)
            dv = dot(gt, pb)
            if first is None:
                dkt[:, keys] = dk
                dvt[:, keys] = dv
            else:
                dkt[:, keys] = dkt[:, keys] + dk
                dvt[:, keys] = dvt[:, keys] + dv

        def copy_in(row, rows, slot):
            return pltpu.make_async_copy(
                p.at[h, pl.ds(row, rows), :],
                pbuf.at[slot, pl.ds(0, rows), :],
                psem.at[slot],
            )

        copy_in(0, QB, 0).start()
        dkt[:, :LONGEST] = jnp.zeros((HEAD, LONGEST), F32)
        dvt[:, :LONGEST] = jnp.zeros((HEAD, LONGEST), F32)

        def step(b, _):
            row = pl.multiple_of(b * QB, QB)
            slot = lax.rem(b, 2)

            @pl.when(b < whole - 1)
            def _():
                copy_in(row + QB, QB, 1 - slot).start()

            @pl.when(b == whole - 1)
            def _():
                copy_in(whole * QB, rest, whole % 2).start()

            copy_in(row, QB, slot).wait()
            block(
                row,
                QB,
                row // own,
                pl.multiple_of(row % own, QB),
                pbuf[slot],
                slice(0, LONGEST),
                0,
            )
            return 0

        lax.fori_loop(0, whole, step, 0)
        row = whole * QB
        copy_in(row, rest, whole % 2).wait()
        block(row, rest, row // own, row % own, pbuf[whole % 2, :rest], slice(0, LONGEST), 0)
        block(
            LONGEST,
            tail,
            LONGEST // own,
            LONGEST % own,
            p2[h],
            slice(LONGEST, group),
            None,
        )
        for c in range(0, group, own):
            d[c // own, 1, :, hs] = dkt[:, c : c + own].T.astype(BF)
            d[c // own, 2, :, hs] = dvt[:, c : c + own].T.astype(BF)


def norm_parts(r):
    centre = r - jnp.mean(r, axis=-1, keepdims=True)
    spread = jnp.mean(centre * centre, axis=-1, keepdims=True)
    rstd = lax.rsqrt(spread + 1e-05)
    return centre * rstd, rstd


def norm_back(dn, n, rstd):
    return rstd * (
        dn - jnp.mean(dn, axis=-1, keepdims=True) - n * jnp.mean(dn * n, axis=-1, keepdims=True)
    )


def colsum(a):
    return jnp.sum(a, axis=0, keepdims=True)


def flip(a):
    return a.astype(F32).T.astype(BF)


GELU_C = 0.7978845608
GELU_A = 0.044715


def middle(
    attn, x, cot, wout, small, bgu, w,
    result, dsum1, dattn, gw, gwout, gsmall, gbgu,
    mid, midb, midt, gate, up, y, dffn, dffnt, dmid,
):
    i = pl.program_id(0)
    n = pl.num_programs(0) // 2
    parts = attn.shape[0]

    @pl.when(i == 0)
    def _():
        branch = x[...].astype(F32) + small[2:3, :]
        for r in range(parts):
            branch += dot_nt(attn[r], wout[r])
        nn, _ = norm_parts(branch)
        m = nn * small[3:4, :] + small[4:5, :]
        dsum1[...] = branch
        mid[...] = m
        midb[...] = m.astype(BF)
        midt[...] = m.T.astype(BF)
        y[...] = jnp.zeros_like(y)

    @pl.when(i < n)
    def _():
        mb = midb[...]
        ga = dot(mb, w[0, 0]) + bgu[0, 0:1, :]
        u = dot(mb, w[1, 0]) + bgu[0, 1:2, :]
        gate[i] = ga
        up[i] = u
        t = jnp.tanh(GELU_C * (ga + GELU_A * ga * ga * ga))
        act = (0.5 * ga * (1.0 + t) * u).astype(BF)
        y[...] += dot_nt(act, w[2, 0])

    @pl.when(i == n - 1)
    def _():
        r = mid[...] + y[...] + small[5:6, :]
        nn, rstd = norm_parts(r)
        gain = small[6:7, :]
        result[...] = (nn * gain + small[7:8, :]).astype(BF)
        c = cot[...].astype(F32)
        ds = norm_back(c * gain, nn, rstd)
        gsmall[6:7, :] = colsum(c * nn)
        gsmall[7:8, :] = colsum(c)
        dmid[...] = ds
        db = ds.astype(BF)
        dffn[...] = db
        dffnt[...] = ds.T.astype(BF)
        gsmall[5:6, :] = colsum(db.astype(F32))
        gsmall[0:2, :] = jnp.zeros_like(gsmall[0:2, :])

    @pl.when(i >= n)
    def _():
        k = 2 * n - 1 - i
        ga = gate[k]
        u = up[k]
        sq = ga * ga
        t = jnp.tanh(GELU_C * (ga + GELU_A * ga * sq))
        half = 0.5 * (1.0 + t)
        gelu = ga * half
        slope = half + (0.5 * GELU_C) * ga * (1.0 - t * t) * (1.0 + 3.0 * GELU_A * sq)
        act = (gelu * u).astype(BF)
        dact = dot(dffn[...], w[2, 0])
        gw[0, 2] = dot(dffnt[...], act).astype(BF)
        dga = (dact * u * slope).astype(BF)
        du = (dact * gelu).astype(BF)
        gbgu[0, 0:1, :] = colsum(dga.astype(F32))
        gbgu[0, 1:2, :] = colsum(du.astype(F32))
        gw[0, 0] = dot(midt[...], dga).astype(BF)
        gw[0, 1] = dot(midt[...], du).astype(BF)
        dmid[...] += dot_nt(dga, w[0, 0]) + dot_nt(du, w[1, 0])

    @pl.when(i == 2 * n - 1)
    def _():
        nn, rstd = norm_parts(dsum1[...])
        dm = dmid[...]
        gsmall[3:4, :] = colsum(dm * nn)
        gsmall[4:5, :] = colsum(dm)
        ds = norm_back(dm * small[3:4, :], nn, rstd)
        dsum1[...] = ds
        db = ds.astype(BF)
        gsmall[2:3, :] = colsum(db.astype(F32))
        dbt = ds.T.astype(BF)
        for r in range(parts):
            dattn[r] = dot(db, wout[r]).astype(BF)
            gwout[r] = dot(dbt, attn[r]).astype(BF)


def head_slopes(first_head, head_count):
    number = first_head + jnp.arange(head_count, dtype=jnp.int32)
    exponent = jnp.where(number < 8, number.astype(F32) + 1.0, number.astype(F32) - 7.5)
    return jnp.exp2(-exponent)


def params(**kw):
    return pltpu.CompilerParams(vmem_limit_bytes=VMEM_LIMIT, **kw)


def per_device(
    hidden_in, lengths, w_qkv, b_qv, w_out, b_out, ln1_gain, ln1_bias, w_gu, b_gu, w_down,
    b_down, ln2_gain, ln2_bias, cotangent,
):
    both = ("dp", "mp")
    n_dp, n_mp = lax.axis_size("dp"), lax.axis_size("mp")
    n = n_dp * n_mp
    mp_rank = lax.axis_index("mp")
    own, width = hidden_in.shape
    group = own * n_mp
    sds = jax.ShapeDtypeStruct

    small_own = jnp.concatenate(
        [b_qv, jnp.stack([b_out, ln1_gain, ln1_bias, b_down, ln2_gain, ln2_bias])], axis=0
    )
    small_flat = jnp.concatenate([small_own.reshape(1, -1), b_gu.reshape(1, -1)], axis=1)
    small_all = lax.all_gather(small_flat, both, axis=0, tiled=True)
    cut = small_own.size
    small = small_all[:, :cut].reshape(n, 8, -1).transpose(1, 0, 2).reshape(8, width)
    bgu = small_all[:, cut:].reshape(n, 2, -1).transpose(1, 0, 2).reshape(2, n_mp, -1)
    bgu = bgu.transpose(1, 0, 2)
    ff_part = bgu.shape[2]

    wq = w_qkv.astype(BF)
    wq_own = lax.all_gather(wq, "dp", axis=1, tiled=True)
    hid = lax.all_gather(hidden_in, "mp", axis=0, tiled=True)
    cols = wq.shape[2]
    heads = cols // HEAD

    attn_pack = jnp.concatenate([wq[0], wq[1], wq[2], w_out.T.astype(BF)], axis=1)
    pack = jnp.concatenate([w_gu.astype(BF), w_down.T.astype(BF)[None], attn_pack[None]], axis=0)
    weights = lax.all_gather(pack, ("mp", "dp"), axis=1, tiled=True)
    weights = weights.reshape(4, n_mp, width, ff_part)
    wqkv_full = weights[3, :, :, : 3 * cols]
    wout_full = weights[3, :, :, 3 * cols :]

    qv_bias = lax.dynamic_slice_in_dim(small[:2], mp_rank * cols, cols, 1)
    qkv_bias = jnp.stack([qv_bias[0], jnp.zeros_like(qv_bias[0]), qv_bias[1]])
    slopes = head_slopes(mp_rank * heads, heads)
    tail = group - LONGEST

    qkv, o, u, p, p2 = pl.pallas_call(
        attention_forward,
        out_shape=(
            sds((3, group, cols), BF),
            sds((n_mp, own, cols), BF),
            sds((heads, group, 2 * HEAD), F32),
            sds((heads, LONGEST, LONGEST), BF),
            sds((heads, tail, tail), BF),
        ),
        in_specs=[vmem(), vmem(), vmem(), smem(), smem()],
        out_specs=(vmem(), vmem(), vmem(), hbm(), vmem()),
        scratch_shapes=[
            pltpu.VMEM((cols, group), BF),
            pltpu.VMEM((heads, group, 2 * HEAD), BF),
            pltpu.VMEM((QB, LONGEST + LONGEST // QB * QB), F32),
            pltpu.VMEM((2, QB, LONGEST), BF),
            pltpu.SemaphoreType.DMA((2,)),
        ],
        compiler_params=params(),
        name="attention_forward",
    )(hid, wq_own, qkv_bias, slopes, lengths)

    attn = lax.all_to_all(o, "mp", 0, 0, tiled=True)

    fixed = lambda *s: pl.BlockSpec(s, lambda i: (0,) * len(s))
    walk = lambda i: jnp.where(i < n_mp, i, 2 * n_mp - 1 - i)
    back = lambda i: jnp.where(i < n_mp, n_mp - 1, 2 * n_mp - 1 - i)
    result, dsum1, dattn, gw, gwout, gsmall, gbgu = pl.pallas_call(
        middle,
        grid=(2 * n_mp,),
        out_shape=(
            sds((own, width), BF),
            sds((own, width), F32),
            sds((n_mp, own, cols), BF),
            sds((n_mp, 3, width, ff_part), BF),
            sds((n_mp, width, cols), BF),
            sds((8, width), F32),
            sds((n_mp, 2, ff_part), F32),
        ),
        in_specs=[
            fixed(n_mp, own, cols),
            fixed(own, width),
            fixed(own, width),
            fixed(n_mp, width, cols),
            fixed(8, width),
            pl.BlockSpec((1, 2, ff_part), lambda i: (walk(i), 0, 0)),
            pl.BlockSpec((3, 1, width, ff_part), lambda i: (0, walk(i), 0, 0)),
        ],
        out_specs=(
            fixed(own, width),
            fixed(own, width),
            fixed(n_mp, own, cols),
            pl.BlockSpec((1, 3, width, ff_part), lambda i: (back(i), 0, 0, 0)),
            fixed(n_mp, width, cols),
            fixed(8, width),
            pl.BlockSpec((1, 2, ff_part), lambda i: (back(i), 0, 0)),
        ),
        scratch_shapes=[
            pltpu.VMEM((own, width), F32),
            pltpu.VMEM((own, width), BF),
            pltpu.VMEM((width, own), BF),
            pltpu.VMEM((n_mp, own, ff_part), F32),
            pltpu.VMEM((n_mp, own, ff_part), F32),
            pltpu.VMEM((own, width), F32),
            pltpu.VMEM((own, width), BF),
            pltpu.VMEM((width, own), BF),
            pltpu.VMEM((own, width), F32),
        ],
        compiler_params=params(),
        name="middle",
    )(attn, hidden_in, cotangent, wout_full, small, bgu, weights[:3])

    g = lax.all_to_all(dattn, "mp", 0, 0, tiled=True)

    d = pl.pallas_call(
        attention_backward,
        out_shape=sds((n_mp, 3, own, cols), BF),
        in_specs=[vmem(), vmem(), vmem(), hbm(), vmem()],
        out_specs=vmem(),
        scratch_shapes=[
            pltpu.VMEM((heads, 2 * HEAD, group), BF),
            pltpu.VMEM((2, QB, LONGEST), BF),
            pltpu.VMEM((HEAD, group), F32),
            pltpu.VMEM((HEAD, group), F32),
            pltpu.SemaphoreType.DMA((2,)),
        ],
        compiler_params=params(),
        name="attention_backward",
    )(qkv, g, u, p, p2)

    dl = lax.all_to_all(d, "mp", 0, 0, tiled=True)
    grad_in = (
        dsum1
        + jnp.einsum(
            "rstc,rdsc->td",
            dl,
            wqkv_full.reshape(n_mp, width, 3, cols),
            preferred_element_type=F32,
        )
    ).astype(BF)
    gqkv = jnp.einsum(
        "rtd,rstc->sdc", hid.reshape(n_mp, own, width), d, preferred_element_type=F32
    ).astype(BF)
    sums = jnp.sum(d.astype(F32), axis=(0, 2))
    gqv = lax.dynamic_update_slice_in_dim(
        gsmall[:2], jnp.stack([sums[0], sums[2]]), mp_rank * cols, 1
    )
    gsmall = jnp.concatenate([gqv, gsmall[2:]], axis=0)

    gsmall = gsmall.reshape(8, n, -1).transpose(1, 0, 2).reshape(n, -1)
    gbgu = gbgu.transpose(1, 0, 2).reshape(2, n, -1).transpose(1, 0, 2).reshape(n, -1)
    gall = jnp.concatenate([gsmall, gbgu], axis=1)
    gown = lax.psum_scatter(gall, both, scatter_dimension=0, tiled=True)
    gs = gown[0, :cut].reshape(8, -1)
    g_gu = gown[0, cut:].reshape(2, -1)

    gqkv = lax.psum_scatter(gqkv, "dp", scatter_dimension=1, tiled=True).astype(F32)
    gw = lax.psum_scatter(gw, "dp", scatter_dimension=2, tiled=True)
    gw = gw.reshape(-1, ff_part)
    gw = lax.psum_scatter(gw, "mp", scatter_dimension=0, tiled=True).reshape(3, -1, ff_part)
    gwout = lax.psum_scatter(gwout, "dp", scatter_dimension=1, tiled=True)
    gwout = lax.psum_scatter(gwout, "mp", scatter_dimension=0, tiled=True)[0]
    return (
        result,
        grad_in,
        gqkv,
        gs[0:2],
        gwout.T.astype(F32),
        gs[2],
        gs[3],
        gs[4],
        gw[:2].astype(F32),
        g_gu,
        gw[2].T.astype(F32),
        gs[5],
        gs[6],
        gs[7],
    )


def solution(mesh):
    rows = P(("dp", "mp"), None)
    vec = P(("dp", "mp"))
    vecs = P(None, ("dp", "mp"))
    wide = P(None, "dp", "mp")
    tall = P("mp", "dp")
    return jax.shard_map(
        per_device,
        mesh=mesh,
        in_specs=(
            rows, P("dp", None), wide, vecs, tall, vec, vec, vec, wide, vecs, tall, vec, vec, vec,
            rows,
        ),
        out_specs=(
            rows, rows, wide, vecs, tall, vec, vec, vec, wide, vecs, tall, vec, vec, vec,
        ),
        check_vma=False,
    )
```

time: 998 us -> 531 us (0.53)
  matrix products: 206 us -> 10.6 us
  waiting for transfers between devices: 332 us -> 166 us
  Pallas kernels: 0 us -> 110 us
  other arithmetic: 105 us -> 9.35 us
  blocking collectives: 243 us -> 148 us
  local copies, waits for them, and re-layouts: 70.4 us -> 53.3 us
  loops' own time: 16.6 us -> 0 us
    dot_general x40 -> x2, matrix products: 206 us -> 10.6 us  [the longest x1 5.64 us: per_device(): jnp.einsum('rstc,rdsc->td', dl, wqkv_full.reshape(n_mp, width, 3, cols),...]
    reduce_scatter x5 -> x4, waiting for transfers between devices: 211 us -> 90.1 us  [the longest x1 57.1 us: per_device(): gw = lax.psum_scatter(gw, 'dp', scatter_dimension=2, tiled=True)]
    pallas_call x0 -> x3, Pallas kernels: none -> 110 us  [the longest x1 39.7 us: per_device(): pl.pallas_call(middle, grid=(2 * n_mp,), out_shape=(sds((own, width), BF)...]
    all_gather x4 -> x2, blocking collectives: 162 us -> 85.5 us  [the longest x1 71.9 us: per_device(): small_all = lax.all_gather(small_flat, both, axis=0, tiled=True)]
    all_gather x6 -> x2, waiting for transfers between devices: 95.4 us -> 32 us  [the longest x1 32 us: per_device(): weights = lax.all_gather(pack, ('mp', 'dp'), axis=1, tiled=True)]
    unnamed x2 -> x1, blocking collectives: 81 us -> 39.7 us
    reduce_sum x17 -> x1, other arithmetic: 41 us -> 0.63 us  [per_device(): sums = jnp.sum(d.astype(F32), axis=(0, 2))]
    convert_element_type x22 -> x5, other arithmetic: 45.1 us -> 5.38 us  [the longest x1 1.64 us: per_device(): gw[2].T.astype(F32)]
  transfers between devices with their start and end apart: 15 -> 9, of which waited for: 8 -> 5; matrix products, arithmetic and copies ran while one was open for 25% -> 10% of each run, Pallas kernels for 0% -> 13%
where the time goes in v1:
time: 531 us; the launch traced here: 521 us
  waiting for transfers between devices  166 us (31%)
  blocking collectives  148 us (28%)
  Pallas kernels  110 us (21%)
  local copies, waits for them, and re-layouts  53.3 us (10%)
  between operations  15 us (3%)
  matrix products  10.6 us (2%)
  other arithmetic  9.35 us (2%)
  starting transfers between devices  8.28 us (2%)
    all_gather x1, blocking collectives, per_device(): small_all = lax.all_gather(small_flat, both, axis=0, tiled=True)  71.9 us
    reduce_scatter x1, waiting for transfers between devices, per_device(): gw = lax.psum_scatter(gw, 'dp', scatter_dimension=2, tiled=True)  57.1 us
    unnamed x1, blocking collectives  39.7 us
    pallas_call x1, Pallas kernels, per_device(): pl.pallas_call(middle, grid=(2 * n_mp,), out_shape=(sds((own, width), BF)...  39.7 us
    all_to_all x1, waiting for transfers between devices, per_device(): attn = lax.all_to_all(o, 'mp', 0, 0, tiled=True)  39.5 us
    pallas_call x1, Pallas kernels, per_device(): pl.pallas_call(attention_backward, out_shape=sds((n_mp, 3, own, cols), BF...  37.2 us
    reduce_scatter x1, waiting for transfers between devices, per_device(): lax.psum_scatter(gw, 'mp', scatter_dimension=0, tiled=True)  33 us
    pallas_call x1, Pallas kernels, per_device(): pl.pallas_call(attention_forward, out_shape=(sds((3, group, cols), BF), s...  32.9 us
  transfers between devices with their start and end apart: 9, of which 5 were waited for; matrix products, arithmetic and copies ran while one was open for 10% of the time, Pallas kernels for 13%

profile of v1, /device:TPU:0, one launch (start us, length us, event | category | flops | bytes accessed | tf_op | source)
XLA Modules:
  0.0 520.9 jit_solution(7001004268224242914)
XLA Ops:
  7.3 0.7 all-gather.4.cloned.1.call-update
  8.0 1.0 copy.63
  9.0 1.0 convert_element_type.58
  10.0 1.1 convert_element_type.60
  11.2 1.0 convert_bitcast_fusion.1
  12.2 0.9 pad_maximum_fusion
  13.5 71.9 %all-gather = f32[32,1,384]{2,1,0:T(1,128)S(1)} all-gather(f32[1,1,384]{2,1,0:T(1,128)S(1)} %maximum_bitcast_fusion.1), channel_id=1, replica_groups=mesh['dp'=8,'mp'=4] {'dp','mp'}, dimensions={0}, use_global_device_ids=true | all-gather | bytes 50688 | tf_op jit(solution)/shard_map/all_gather | solution.py:374
  86.4 13.5 %all_gather.13.w = bf16[3,768,192]{2,1,0:T(8,128)(2,1)} all-gather(bf16[3,96,192]{2,1,0:T(8,128)(2,1)S(1)} %convert_element_type.58), channel_id=1, replica_groups=mesh['dp'=8,'mp'=4] {'dp'}, dimensions={1}, use_global_device_ids=true | all-gather | bytes 995328 | tf_op jit(solution)/shard_map/all_gather | solution.py:382
  99.9 0.7 pad_maximum_fusion.3.bias
  100.6 32.9 %attention_forward.1 = (bf16[3,2048,192]{2,1,0:T(8,128)(2,1)}, bf16[4,512,192]{2,1,0:T(8,128)(2,1)}, f32[3,2048,128]{2,1,0:T(8,128)}, bf16[3,1664,1664]{2,1,0:T(8,128)(2,1)}, bf16[3,384,384]{2,1,0:T(8,128)(2,1)}) custom-call(bf16[2048,768]{1,0:T(8,128)(2,1)} %all-gather.4.cloned.1.call-done.x, bf16[3,768,192]{2,1,0:T(8,128)(2,1)} %all_gather.13.w, ...), custom_call_target="tpu_custom_call" | custom-call | tf_op jit(solution)/shard_map/attention_forward/pallas_call | solution.py:399
  133.6 2.2 copy.62
  135.8 3.5 all-to-all-start
  139.5 0.6 copy.87
  140.1 0.7 reshape.94.small
  140.9 39.5 %all-to-all-done = bf16[4,512,192]{1,2,0:T(8,128)(2,1)S(1)} async-done(((bf16[4,512,192]{1,2,0:T(8,128)(2,1)}), bf16[4,512,192]{1,2,0:T(8,128)(2,1)S(1)}, u32[]{:S(2)}, u32[]{:S(2)}) %all-to-all-start) | async-done | bytes 786464 | tf_op jit(solution)/shard_map/all_to_all | solution.py:421
  180.4 1.3 copy.67.attn
  181.7 32.0 %all-gather.6.cloned.1.call-done = bf16[4,3072,768]{2,1,0:T(8,128)(2,1)} async-done(((bf16[4,96,768]{2,1,0:T(8,128)(2,1)}), bf16[4,3072,768]{2,1,0:T(8,128)(2,1)}) %all-gather.6.cloned.1.call-update) | async-done | bytes 18874384 | tf_op jit(solution)/shard_map/all_gather | solution.py:389
  213.7 3.3 slice_bitcast_fusion.wout
  216.9 12.8 %slice.135 = bf16[3,3072,768]{2,1,0:T(8,128)(2,1)} slice(bf16[4,3072,768]{2,1,0:T(8,128)(2,1)} %all-gather.6.cloned.1.call-done), slice={[0:3], [0:3072], [0:768]} | slice | bytes 28311552 | tf_op jit(solution)/shard_map/slice | solution.py:469
  229.8 39.7 %middle.1 = (bf16[512,768]{1,0:T(8,128)(2,1)}, f32[512,768]{1,0:T(8,128)}, bf16[4,512,192]{2,1,0:T(8,128)(2,1)}, bf16[4,3,768,768]{3,2,1,0:T(8,128)(2,1)}, bf16[...) custom-call(bf16[4,512,192]{2,1,0:T(8,128)(2,1)} %copy.67.attn, bf16[512,768]{1,0:T(8,128)(2,1)} %x.1, ...), custom_call_target="tpu_custom_call" | custom-call | tf_op jit(solution)/shard_map/middle/pallas_call | solution.py:426
  270.1 0.6 copy-done.3
  270.7 0.7 copy.68
  271.4 23.2 %all_to_all.15 = bf16[4,512,192]{1,2,0:T(8,128)(2,1)S(1)} all-to-all(bf16[4,512,192]{1,2,0:T(8,128)(2,1)S(1)} %copy.68), channel_id=1, replica_groups=mesh['dp'=8,'mp'=4] {'mp'}, dimensions={0} | all-to-all | bytes 1572864 | tf_op jit(solution)/shard_map/all_to_all | solution.py:471
  294.7 1.3 copy.69.g
  296.0 37.2 %attention_backward.1 = bf16[4,3,512,192]{3,2,1,0:T(8,128)(2,1)} custom-call(bf16[3,2048,192]{2,1,0:T(8,128)(2,1)} %get-tuple-element.29.qkv, bf16[4,512,192]{2,1,0:T(8,128)(2,1)} %copy.69.g, f32[3,2048,128]{2,1,0:T(8,128)} %get-tuple-element.31.u, bf16[3,1664,1664]{2,1,0:T(8,128)(2,1)} %get-tuple-element.32.p, bf16[3,384,384]{2,1,0:T(8,128)(2,1)} %get-tuple-element.33.p2), custom_call_target="tpu_custom_call" | custom-call | tf_op jit(solution)/shard_map/attention_backward/pallas_call | solution.py:473
  333.3 4.9 fusion.1
  338.2 3.7 copy.81
  341.9 4.1 reshape.110
  346.0 2.7 copy.70
  348.7 4.5 all-to-all-start.2
  353.3 57.1 %reduce-scatter.12.cloned.1.call-done = bf16[4,3,96,768]{3,2,1,0:T(8,128)(2,1)} async-done(((bf16[4,3,768,768]{3,2,1,0:T(8,128)(2,1)}), bf16[4,3,96,768]{3,2,1,0:T(8,128)(2,1)}) %reduce-scatter.12.cloned.1.call-update) | async-done | bytes 1769488 | tf_op jit(solution)/shard_map/reduce_scatter | solution.py:516
  410.4 4.4 slice.136
  414.8 6.4 %copy.71 = bf16[1,4,768,576]{2,3,1,0:T(8,128)(2,1)} copy(bf16[1,4,768,576]{3,2,1,0:T(8,128)(2,1)} %slice.136) | data formatting | bytes 7077888 | tf_op jit(solution)/shard_map/slice | solution.py:391
  421.5 0.6 convert_reduce_fusion
  422.7 39.7 %all-reduce = f32[32,384]{1,0:T(8,128)S(1)} all-reduce(f32[32,384]{1,0:T(8,128)S(1)} %pad_maximum_fusion.1), channel_id=3, replica_groups=mesh['dp'=8,'mp'=4] {'dp','mp'}, use_global_device_ids=true, to_apply=%region_2.3.clone | all-reduce | flops 12288 | bytes 98304
  462.6 0.6 reshape_squeeze.8
  463.2 0.6 slice.118
  463.9 0.6 dynamic-slice_bitcast_fusion
  464.5 0.8 convert_bitcast_fusion.2
  465.3 0.7 copy.77
  466.0 3.4 reduce-scatter.16.cloned.1.call-done
  469.4 1.0 reshape.111
  470.6 0.9 copy.76
  471.5 5.6 %fusion = bf16[512,768]{1,0:T(8,128)(2,1)} fusion(f32[512,768]{1,0:T(8,128)S(1)} %copy-done.2, bf16[4,3,512,192]{2,3,1,0:T(8,128)(2,1)} %all-to-all-done.2, bf16[4,768,3,192]{1,3,2,0:T(8,128)(2,1)} %bitcast.89), kind=kOutput, calls=%fused_computation.4 | convolution fusion | flops 1812725760 | bytes 8257536 | tf_op jit(solution)/shard_map/rstc,rdsc->td/dot_general | solution.py:492
  477.2 33.0 %reduce-scatter.14.cloned.1.call-done = bf16[288,768]{1,0:T(8,128)(2,1)} async-done(((bf16[1152,768]{1,0:T(8,128)(2,1)}), bf16[288,768]{1,0:T(8,128)(2,1)}) %reduce-scatter.14.cloned.1.call-update) | async-done | bytes 442384 | tf_op jit(solution)/shard_map/reduce_scatter | solution.py:518
  510.2 1.0 slice.139
  511.1 0.9 convert.5
  512.0 1.6 convert_bitcast_fusion
  (80 shorter events, 3.6 us)
Async XLA Ops:
  7.2 6.0 %copy-start.6 = (f32[2,96]{1,0:T(2,128)S(1)}, f32[2,96]{1,0:T(2,128)}, u32[]{:S(2)}) copy-start(f32[2,96]{1,0:T(2,128)} %param.24) | copy-start | bytes 2308
  7.2 6.0 %copy-start.13 = (f32[24]{0:T(128)S(1)}, f32[24]{0:T(128)}, u32[]{:S(2)}) copy-start(f32[24]{0:T(128)} %param.28) | copy-start | bytes 292
  7.2 6.0 %copy-start.12 = (f32[24]{0:T(128)S(1)}, f32[24]{0:T(128)}, u32[]{:S(2)}) copy-start(f32[24]{0:T(128)} %param.27) | copy-start | bytes 292
  7.2 6.0 %copy-start.11 = (f32[24]{0:T(128)S(1)}, f32[24]{0:T(128)}, u32[]{:S(2)}) copy-start(f32[24]{0:T(128)} %param.26) | copy-start | bytes 292
  7.2 6.0 %copy-start.10 = (f32[24]{0:T(128)S(1)}, f32[24]{0:T(128)}, u32[]{:S(2)}) copy-start(f32[24]{0:T(128)} %param.22) | copy-start | bytes 292
  7.2 6.0 %copy-start.9 = (f32[24]{0:T(128)S(1)}, f32[24]{0:T(128)}, u32[]{:S(2)}) copy-start(f32[24]{0:T(128)} %param.21) | copy-start | bytes 292
  7.2 6.0 %copy-start.8 = (f32[24]{0:T(128)S(1)}, f32[24]{0:T(128)}, u32[]{:S(2)}) copy-start(f32[24]{0:T(128)} %param.20) | copy-start | bytes 292
  7.3 6.0 %copy-start.7 = (f32[2,24]{1,0:T(2,128)S(1)}, f32[2,24]{1,0:T(2,128)}, u32[]{:S(2)}) copy-start(f32[2,24]{1,0:T(2,128)} %param.18) | copy-start | bytes 580
  7.3 93.3 %all-gather.4.cloned.1.call-start = ((), (), s32[]{:S(2)}) async-start(), calls=%async_computation.8 | async-start | bytes 3932160 | tf_op jit(solution)/shard_map/all_gather | solution.py:383
  8.0 205.7 %all-gather.6.cloned.1.call-start = ((), (), s32[]{:S(2)}) async-start(), calls=%async_computation.9 | async-start | bytes 19464192 | tf_op jit(solution)/shard_map/all_gather | solution.py:389
  135.8 44.6 %all-to-all-start = ((bf16[4,512,192]{1,2,0:T(8,128)(2,1)}), bf16[4,512,192]{1,2,0:T(8,128)(2,1)S(1)}, u32[]{:S(2)}, u32[]{:S(2)}) async-start(bf16[4,512,192]{1,2,0:T(8,128)(2,1)} %copy.62), calls=%async_computation | async-start | bytes 1572864 | tf_op jit(solution)/shard_map/all_to_all | solution.py:421
  139.3 193.9 %reduce-scatter.8.cloned.1.call-start = ((), (), s32[]{:S(2)}) async-start(), calls=%async_computation.10 | async-start | bytes 1769472 | tf_op jit(solution)/shard_map/reduce_scatter | solution.py:519
  269.5 140.9 %reduce-scatter.12.cloned.1.call-start = ((), (), s32[]{:S(2)}) async-start(), calls=%async_computation.12 | async-start | bytes 15925248 | tf_op jit(solution)/shard_map/reduce_scatter | solution.py:516
  269.5 1.2 copy-start.3
  270.0 194.5 %reduce-scatter.10.cloned.1.call-start = ((), (), s32[]{:S(2)}) async-start(), calls=%async_computation.11 | async-start | bytes 245760 | tf_op jit(solution)/shard_map/reduce_scatter | solution.py:520
  296.0 37.3 %copy-start.1 = (bf16[2048,768]{1,0:T(8,128)(2,1)S(1)}, bf16[2048,768]{1,0:T(8,128)(2,1)}, u32[]{:S(2)}) copy-start(bf16[2048,768]{1,0:T(8,128)(2,1)} %all-gather.4.cloned.1.call-done.x) | copy-start | bytes 9437188
  333.2 136.2 %reduce-scatter.16.cloned.1.call-start = ((), (), s32[]{:S(2)}) async-start(), calls=%async_computation.14 | async-start | bytes 1105920
  338.2 7.8 %copy-start = (bf16[4,3,512,192]{3,2,1,0:T(8,128)(2,1)S(1)}, bf16[4,3,512,192]{3,2,1,0:T(8,128)(2,1)}, u32[]{:S(2)}) copy-start(bf16[4,3,512,192]{3,2,1,0:T(8,128)(2,1)} %attention_backward.1) | copy-start | bytes 7077892
  348.7 122.8 %all-to-all-start.2 = ((bf16[4,3,512,192]{2,3,1,0:T(8,128)(2,1)}), bf16[4,3,512,192]{2,3,1,0:T(8,128)(2,1)}, u32[]{:S(2)}, u32[]{:S(2)}) async-start(bf16[4,3,512,192]{2,3,1,0:T(8,128)(2,1)} %copy.70), calls=%async_computation.2 | async-start | bytes 4718592 | tf_op jit(solution)/shard_map/all_to_all | solution.py:489
  353.2 156.9 %reduce-scatter.14.cloned.1.call-start = ((), (), s32[]{:S(2)}) async-start(), calls=%async_computation.13 | async-start | bytes 2211840 | tf_op jit(solution)/shard_map/reduce_scatter | solution.py:518
  410.4 4.4 copy-start.4
  414.8 6.4 %copy-start.5 = (f32[4,2,768]{2,1,0:T(2,128)S(1)}, f32[4,2,768]{2,1,0:T(2,128)}, u32[]{:S(2)}) copy-start(f32[4,2,768]{2,1,0:T(2,128)} %get-tuple-element.35) | copy-start | bytes 73732
  422.1 49.4 %copy-start.2 = (f32[512,768]{1,0:T(8,128)S(1)}, f32[512,768]{1,0:T(8,128)}, u32[]{:S(2)}) copy-start(f32[512,768]{1,0:T(8,128)} %get-tuple-element.28) | copy-start | bytes 4718596
Sparse Core Ops, SparseCore 0:
  9.7 66.7 all-gather.3
  80.0 133.6 all-gather.5
  269.6 36.5 reduce-scatter.7
  309.6 100.7 reduce-scatter.11
  412.5 19.3 reduce-scatter.9
  435.3 34.0 reduce-scatter.15
  471.7 38.3 reduce-scatter.13

commit v2 on v1

v2 whole, which is shorter than its diff:
```python
import functools

import jax
import jax.numpy as jnp
from jax import lax
from jax.experimental import pallas as pl
from jax.experimental.pallas import tpu as pltpu
from jax.sharding import PartitionSpec as P

HEAD = 64
LONGEST = 1664
QB = 256
BF = jnp.bfloat16
F32 = jnp.float32
VMEM_LIMIT = 60 * 1024 * 1024


def dot(a, b):
    return lax.dot_general(a, b, (((1,), (0,)), ((), ())), preferred_element_type=F32)


def dot_nt(a, b):
    return lax.dot_general(a, b, (((1,), (1,)), ((), ())), preferred_element_type=F32)


def vmem():
    return pl.BlockSpec(memory_space=pltpu.VMEM)


def smem():
    return pl.BlockSpec(memory_space=pltpu.SMEM)


def hbm():
    return pl.BlockSpec(memory_space=pl.ANY)


MESH = pl.DeviceIdType.MESH
PIECES = 4


def greet(n_dp, n_mp, me_dp, me_mp):
    barrier = pltpu.get_barrier_semaphore()
    for j in range(1, n_mp):
        pl.semaphore_signal(
            barrier, 1, device_id=(me_dp, lax.rem(me_mp + j, n_mp)), device_id_type=MESH
        )
    for j in range(1, n_dp):
        pl.semaphore_signal(
            barrier, 1, device_id=(lax.rem(me_dp + j, n_dp), me_mp), device_id_type=MESH
        )
    pl.semaphore_wait(barrier, n_mp - 1 + n_dp - 1)


def front(
    n_dp, n_mp,
    x, wq, sin, slope, length,
    small, xt, qt, kp, vte, ut, attnt, p, p2,
    hid, wslot, wf, wb, slot1, ssum, slot2, bias, qs, kt, vext, dist, pbuf, obuf, land,
    hs_sem, hr_sem, ws_sem, wr_sem, s1s, s1r, s2s, s2r, os_sem, or_sem, psem,
):
    me_dp, me = lax.axis_index("dp"), lax.axis_index("mp")
    own = x.shape[0]
    group = own * n_mp
    wrows, cols = wq.shape[1], wq.shape[2]
    heads = cols // HEAD
    tail = group - LONGEST
    full = LONGEST // own
    rest = LONGEST - full * own
    piece = own // PIECES

    def across_mp(j, src, dst, ss, rs):
        to = lax.rem(me + j, n_mp)
        return pltpu.make_async_remote_copy(
            src_ref=src, dst_ref=dst, send_sem=ss, recv_sem=rs,
            device_id=(me_dp, to), device_id_type=MESH,
        )

    def across_dp(j, src, dst, ss, rs):
        to = lax.rem(me_dp + j, n_dp)
        return pltpu.make_async_remote_copy(
            src_ref=src, dst_ref=dst, send_sem=ss, recv_sem=rs,
            device_id=(to, me), device_id_type=MESH,
        )

    greet(n_dp, n_mp, me_dp, me)

    send1 = [across_mp(j, sin, slot1.at[j], s1s.at[j], s1r.at[j]) for j in range(1, n_mp)]
    sendw = [across_dp(j, wq, wslot.at[j], ws_sem.at[j], wr_sem.at[j]) for j in range(1, n_dp)]
    send2 = [across_dp(j, ssum, slot2.at[j], s2s.at[j], s2r.at[j]) for j in range(1, n_dp)]
    for c in send1 + sendw:
        c.start()

    def hidden(way, step, k):
        shard = me - step if way == 0 else me + step
        to = me + 1 if way == 0 else me - 1
        shard, to = jnp.clip(shard, 0, n_mp - 1), jnp.clip(to, 0, n_mp - 1)
        rows = pl.ds(k * piece, piece)
        src = x.at[rows, :] if step == 0 else hid.at[shard, rows, :]
        return pltpu.make_async_remote_copy(
            src_ref=src, dst_ref=hid.at[shard, rows, :],
            send_sem=hs_sem.at[way, step, k], recv_sem=hr_sem.at[way, step, k],
            device_id=(me_dp, to), device_id_type=MESH,
        )

    def sends(way, step):
        if way == 0:
            return (me >= step) & (me < n_mp - 1)
        return (me + step <= n_mp - 1) & (me > 0)

    def receives(way, step):
        return me - 1 - step >= 0 if way == 0 else me + 1 + step <= n_mp - 1

    def send_hidden(step, k):
        for way in range(2):

            @pl.when(sends(way, step))
            def _():
                hidden(way, step, k).start()

    def wait_hidden(step, k):
        for way in range(2):

            @pl.when(receives(way, step))
            def _():
                hidden(way, step, k).wait_recv()

    for k in range(PIECES):
        send_hidden(0, k)

    width = dist.shape[1]
    base = width - LONGEST
    i = lax.broadcasted_iota(jnp.int32, (QB, width), 0)
    j = lax.broadcasted_iota(jnp.int32, (QB, width), 1)
    dist[...] = jnp.abs(i + base - j).astype(F32)

    total = sin[...]
    for c in send1:
        c.wait_recv()
    for j in range(1, n_mp):
        total += slot1[j]
    ssum[...] = total
    for c in send2:
        c.start()

    for k in range(PIECES):
        wait_hidden(0, k)
        if n_mp > 2:
            send_hidden(1, k)

    for c in sendw:
        c.wait_recv()
    for j in range(n_dp):
        place = pl.multiple_of(lax.rem(me_dp - j + n_dp, n_dp) * wrows, wrows)
        for s in range(3):
            part = wq[s] if j == 0 else wslot[j, s]
            wf[s, pl.ds(place, wrows), :] = part.astype(F32)
    for s in range(3):
        wb[s] = wf[s].astype(BF)

    for c in send2:
        c.wait_recv()
    total = ssum[...]
    for j in range(1, n_dp):
        total += slot2[j]
    small[...] = total
    bias[...] = jnp.zeros_like(bias)
    for r in range(n_mp):

        @pl.when(me == r)
        def _():
            bias[0:2, :] = total[0:2, r * cols : (r + 1) * cols]

    one = jnp.where(lax.broadcasted_iota(jnp.int32, (QB, HEAD), 1) == 0, 1.0, 0.0)
    minus = jnp.where(lax.broadcasted_iota(jnp.int32, (HEAD, QB), 0) < 2, -1.0, 0.0)
    none = jnp.zeros((QB, HEAD), F32)

    def project(ref, shard):
        def part(c, _):
            rows = pl.ds(pl.multiple_of(c * QB, QB), QB)
            at = pl.ds(pl.multiple_of(shard * own + c * QB, QB), QB)
            xc = ref[rows, :]
            xt[:, at] = xc.astype(F32).T.astype(BF)
            q = (dot(xc, wb[0]) + bias[0:1, :]).astype(BF).astype(F32) * HEAD**-0.5
            qs[at, :] = q.astype(BF)
            qt[:, at] = q.T.astype(BF)
            k = dot(xc, wb[1])
            kt[:, at] = k.T.astype(BF)
            v = dot(xc, wb[2]) + bias[1:2, :]
            vt = v.T
            for h in range(heads):
                hs = slice(h * HEAD, (h + 1) * HEAD)
                kp[h, at, :] = jnp.concatenate([k[:, hs], none], axis=1).astype(BF)
                vext[h, at, :] = jnp.concatenate([v[:, hs], one], axis=1).astype(BF)
                vte[h, :, at] = jnp.concatenate([vt[hs], minus], axis=0).astype(BF)
            return 0

        lax.fori_loop(0, own // QB, part, 0)

    project(x, me)
    for step in range(1, n_mp):
        if step > 1:
            for k in range(PIECES):
                wait_hidden(step - 1, k)
                if step < n_mp - 1:
                    send_hidden(step, k)
        for way in range(2):

            @pl.when(receives(way, step - 1))
            def _():
                shard = me - step if way == 0 else me + step
                shard = jnp.clip(shard, 0, n_mp - 1)
                project(hid.at[shard], shard)

    def score_block(h, c, place, rows, sl):
        hs = slice(h * HEAD, (h + 1) * HEAD)
        row = c * own + place
        at = pl.ds(pl.multiple_of(row, 128), rows)
        s = dot(qs[at, hs], kt[hs, :LONGEST])
        off = pl.multiple_of(base - row, 128)
        s = s - sl * dist[:rows, pl.ds(off, LONGEST)]
        m = jnp.max(s, axis=1, keepdims=True)
        pb = jnp.exp(s - m).astype(BF)
        pbuf[h, at, :] = pb
        finish(h, c, place, at, rows, dot(pb, vext[h, :LONGEST, :]))

    def finish(h, c, place, at, rows, uu):
        uut = uu.T
        ut[h, :, at] = uut
        oh = uut[:HEAD] * (1.0 / uut[HEAD : HEAD + 1])
        obuf[c, h * HEAD : (h + 1) * HEAD, pl.ds(place, rows)] = oh.astype(BF)

    def short_block(h, c, sl):
        hs = slice(h * HEAD, (h + 1) * HEAD)
        s = dot(qs[LONGEST:, hs], kt[hs, LONGEST:])
        ii = lax.broadcasted_iota(jnp.int32, (tail, tail), 0)
        jj = lax.broadcasted_iota(jnp.int32, (tail, tail), 1)
        s = s - sl * jnp.abs(ii - jj).astype(F32)
        cut = length[0, 1]
        s = jnp.where((ii < cut) == (jj < cut), s, -1e30)
        m = jnp.max(s, axis=1, keepdims=True)
        pb = jnp.exp(s - m).astype(BF)
        p2[h] = pb
        finish(h, c, rest, pl.ds(LONGEST, tail), tail, dot(pb, vext[h, LONGEST:, :]))

    def out_copy(h, j):
        to = lax.rem(me + j, n_mp)
        hs = pl.ds(h * HEAD, HEAD)
        return pltpu.make_async_remote_copy(
            src_ref=obuf.at[to, hs, :], dst_ref=land.at[j, hs, :],
            send_sem=os_sem.at[h, j], recv_sem=or_sem.at[h, j],
            device_id=(me_dp, to), device_id_type=MESH,
        )

    for h in range(heads):
        sl = slope[h]

        def chunk(j, _):
            c = lax.rem(me + 1 + j, n_mp)

            @pl.when(c < full)
            def _():
                for half in range(own // QB):
                    score_block(h, c, half * QB, QB, sl)

            @pl.when(c == full)
            def _():
                score_block(h, c, 0, rest, sl)
                short_block(h, c, sl)

            @pl.when(j < n_mp - 1)
            def _():
                out_copy(h, j + 1).start()

            return 0

        lax.fori_loop(0, n_mp, chunk, 0)
        pltpu.make_async_copy(pbuf.at[h], p.at[h], psem.at[h]).start()

    attnt[me] = obuf[me]
    for h in range(heads):
        hs = slice(h * HEAD, (h + 1) * HEAD)
        for j in range(1, n_mp):
            out_copy(h, j).wait_recv()
            attnt[lax.rem(me - j + n_mp, n_mp), hs, :] = land[j, hs, :]
    for h in range(heads):
        for j in range(1, n_mp):
            out_copy(h, j).wait_send()
        pltpu.make_async_copy(pbuf.at[h], p.at[h], psem.at[h]).wait()
    for c in send1 + sendw + send2:
        c.wait_send()
    for step in range(n_mp - 1):
        for k in range(PIECES):
            for way in range(2):

                @pl.when(sends(way, step))
                def _():
                    hidden(way, step, k).wait_send()


def back(
    n_dp, n_mp,
    gt, xt, qt, kp, vte, ut, p, p2, weights, dsum1, sin, gw, gwo,
    grad_in, gq, small, gff, gout,
    gl, pbuf, dkt, dvt, dbuf, dland, wfull, gbuf, qland, ssum, slot1, slot2,
    pair, cland, xland, zsum, zland, opair, ocland, oxland, ozsum, ozland,
    gs_sem, gr_sem, qs_sem, qr_sem, ds_sem, dr_sem, ws_sem, wr_sem, s1s, s1r, s2s, s2r,
    psem, wsem, ls_sem, cs_sem, cr_sem, xs_sem, xr_sem, zs_sem, zr_sem,
):
    me_dp, me = lax.axis_index("dp"), lax.axis_index("mp")
    own = gt.shape[2]
    cols = gt.shape[1]
    heads = cols // HEAD
    group = own * n_mp
    tail = group - LONGEST
    full = LONGEST // own
    rest = LONGEST - full * own
    wrows = gq.shape[0]

    def across_mp(j, src, dst, ss, rs):
        to = lax.rem(me + j, n_mp)
        return pltpu.make_async_remote_copy(
            src_ref=src, dst_ref=dst, send_sem=ss, recv_sem=rs,
            device_id=(me_dp, to), device_id_type=MESH,
        )

    def across_dp(j, src, dst, ss, rs):
        to = lax.rem(me_dp + j, n_dp)
        return pltpu.make_async_remote_copy(
            src_ref=src, dst_ref=dst, send_sem=ss, recv_sem=rs,
            device_id=(to, me), device_id_type=MESH,
        )

    def fetch_p(h, j, act):
        c = lax.rem(me - j + n_mp, n_mp)
        slot = lax.rem(h * n_mp + j, 2)

        @pl.when(c < full)
        def _():
            rows = pl.ds(pl.multiple_of(c * own, own), own)
            act(pltpu.make_async_copy(p.at[h, rows, :], pbuf.at[slot], psem.at[slot]))

        @pl.when(c == full)
        def _():
            src = p.at[h, pl.ds(full * own, rest), :]
            act(pltpu.make_async_copy(src, pbuf.at[slot, pl.ds(0, rest), :], psem.at[slot]))

    start, wait = lambda copy: copy.start(), lambda copy: copy.wait()
    fetch_p(0, 0, start)
    fetch_w = pltpu.make_async_copy(weights.at[3], wfull, wsem)

    n_q = n_dp // 2
    me_q, me_c = me_dp // 2, lax.rem(me_dp, 2)
    other = me_dp + 1 - 2 * me_c
    kinds = ((gw, pair, cland, xland, zsum, zland), (gwo, opair, ocland, oxland, ozsum, ozland))

    def rank_of(o):
        return lax.rem(me + 1 + o, n_mp)

    def load_copy(o, t):
        src, own_part = kinds[t][:2]
        return pltpu.make_async_copy(
            src.at[rank_of(o), :, :, me_c], own_part.at[o], ls_sem.at[o, t]
        )

    def pair_up(o, t):
        src, land = kinds[t][0], kinds[t][2]
        return pltpu.make_async_remote_copy(
            src_ref=src.at[rank_of(o), :, :, 1 - me_c], dst_ref=land.at[o],
            send_sem=cs_sem.at[o, t], recv_sem=cr_sem.at[o, t],
            device_id=(other, me), device_id_type=MESH,
        )

    def cross(o, j, t):
        src, land = kinds[t][1], kinds[t][3]
        to = lax.rem(me_q + j, n_q)
        return pltpu.make_async_remote_copy(
            src_ref=src.at[o, :, to], dst_ref=land.at[o, j - 1],
            send_sem=xs_sem.at[o, j, t], recv_sem=xr_sem.at[o, j, t],
            device_id=(to * 2 + me_c, me), device_id_type=MESH,
        )

    def along(o, t):
        src, land = kinds[t][4:]
        return pltpu.make_async_remote_copy(
            src_ref=src.at[o], dst_ref=land.at[o],
            send_sem=zs_sem.at[o, t], recv_sem=zr_sem.at[o, t],
            device_id=(me_dp, rank_of(o)), device_id_type=MESH,
        )

    def add_pair(o):
        for t in range(2):
            own_part, land = kinds[t][1], kinds[t][2]
            load_copy(o, t).wait()
            pair_up(o, t).wait_recv()
            mats = own_part.shape[1]

            def add(i, _):
                a = own_part[o, i // n_q, lax.rem(i, n_q)].astype(F32)
                b = land[o, i // n_q, lax.rem(i, n_q)].astype(F32)
                own_part[o, i // n_q, lax.rem(i, n_q)] = (a + b).astype(BF)
                return 0

            lax.fori_loop(0, mats * n_q, add, 0)
            for j in range(1, n_q):
                cross(o, j, t).start()

    def add_cross(o):
        for t in range(2):
            own_part, land, total = kinds[t][1], kinds[t][3], kinds[t][4]
            for j in range(1, n_q):
                cross(o, j, t).wait_recv()
            for m in range(own_part.shape[1]):
                a = own_part[o, m, me_q].astype(F32)
                for j in range(1, n_q):
                    a += land[o, j - 1, m].astype(F32)
                total[o, m] = a.astype(BF)
            if o < n_mp - 1:
                along(o, t).start()

    for o in range(n_mp):
        for t in range(2):
            load_copy(o, t).start()

    greet(n_dp, n_mp, me_dp, me)

    def grad_copy(h, j):
        hs = pl.ds(h * HEAD, HEAD)
        to = lax.rem(me + j, n_mp)
        return across_mp(
            j, gt.at[to, hs, :], gl.at[j, hs, :], gs_sem.at[h, j], gr_sem.at[h, j]
        )

    for h in range(heads):
        for j in range(1, n_mp):
            grad_copy(h, j).start()
    for o in range(n_mp):
        for t in range(2):
            pair_up(o, t).start()
    fetch_w.start()
    gl[0] = gt[me]

    def query_copy(h, j):
        to = lax.rem(me - j + n_mp, n_mp)
        hs = pl.ds(h * HEAD, HEAD)
        return pltpu.make_async_remote_copy(
            src_ref=dbuf.at[to, 0, hs, :], dst_ref=dland.at[j, 0, hs, :],
            send_sem=qs_sem.at[h, j], recv_sem=qr_sem.at[h, j],
            device_id=(me_dp, to), device_id_type=MESH,
        )

    def pair_copy(h, j):
        to = lax.rem(me - j + n_mp, n_mp)
        hs = pl.ds(h * HEAD, HEAD)
        return pltpu.make_async_remote_copy(
            src_ref=dbuf.at[to, pl.ds(1, 2), hs, :], dst_ref=dland.at[j, pl.ds(1, 2), hs, :],
            send_sem=ds_sem.at[h, j], recv_sem=dr_sem.at[h, j],
            device_id=(me_dp, to), device_id_type=MESH,
        )

    def block(h, j, c, place, rows, pb, keys, add):
        row = c * own + place
        at = pl.ds(pl.multiple_of(row, 128), rows)
        hs = slice(h * HEAD, (h + 1) * HEAD)
        uu = ut[h, :, at]
        inv = 1.0 / uu[HEAD : HEAD + 1]
        gg = gl[j, hs, pl.ds(place, rows)].astype(F32) * inv
        total = jnp.sum(gg * uu[:HEAD], axis=0, keepdims=True) * inv
        high = total.astype(BF).astype(F32)
        low = total - high
        index = lax.broadcasted_iota(jnp.int32, (HEAD, rows), 0)
        extra = jnp.where(index == 0, high, jnp.where(index == 1, low, 0.0))
        gext = jnp.concatenate([gg, extra], axis=0).T.astype(BF)
        dp = dot(gext, vte[h, :, keys])
        ds = (pb.astype(F32) * dp).astype(BF)
        dq = dot(ds, kp[h, keys, :]).T[:HEAD] * (HEAD**-0.5)
        dbuf[c, 0, hs, pl.ds(place, rows)] = dq.astype(BF)
        dk = dot(qt[hs, at], ds)
        dv = dot(gg.astype(BF), pb)
        if add:
            dkt[:, keys] = dkt[:, keys] + dk
            dvt[:, keys] = dvt[:, keys] + dv
        else:
            dkt[:, keys] = dk
            dvt[:, keys] = dv

    pump = [1 + o for o in range(n_mp)]
    for h in range(heads):
        hs = slice(h * HEAD, (h + 1) * HEAD)
        dkt[:, :LONGEST] = jnp.zeros((HEAD, LONGEST), F32)
        dvt[:, :LONGEST] = jnp.zeros((HEAD, LONGEST), F32)

        def chunk(j, _):
            c = lax.rem(me - j + n_mp, n_mp)
            slot = lax.rem(h * n_mp + j, 2)

            @pl.when(j < n_mp - 1)
            def _():
                fetch_p(h, j + 1, start)

            if h < heads - 1:

                @pl.when(j == n_mp - 1)
                def _():
                    fetch_p(h + 1, 0, start)

            @pl.when(j > 0)
            def _():
                grad_copy(h, j).wait_recv()

            fetch_p(h, j, wait)

            keys = slice(0, LONGEST)

            @pl.when(c < full)
            def _():
                for half in range(own // QB):
                    at = pl.ds(half * QB, QB)
                    block(h, j, c, half * QB, QB, pbuf[slot, at, :], keys, True)

            @pl.when(c == full)
            def _():
                block(h, j, c, 0, rest, pbuf[slot, :rest, :], keys, True)
                block(h, j, c, rest, tail, p2[h], slice(LONGEST, group), False)

            @pl.when(j > 0)
            def _():
                query_copy(h, j).start()

            for o in range(n_mp):
                if pump[o] // n_mp == h:

                    @pl.when(j == pump[o] % n_mp)
                    def _():
                        add_pair(o)

            return 0

        lax.fori_loop(0, n_mp, chunk, 0)
        if h == heads - 1:
            add_cross(0)
        for c in range(n_mp):
            dbuf[c, 1, hs, :] = dkt[:, c * own : (c + 1) * own].astype(BF)
            dbuf[c, 2, hs, :] = dvt[:, c * own : (c + 1) * own].astype(BF)
        for j in range(1, n_mp):
            pair_copy(h, j).start()

    ones = jnp.ones((8, own), BF)
    sq = jnp.zeros((8, cols), F32)
    sv = jnp.zeros((8, cols), F32)
    for c in range(n_mp):
        sq += dot_nt(ones, dbuf[c, 0])
        sv += dot_nt(ones, dbuf[c, 2])
    ssum[...] = sin[...]
    for r in range(n_mp):

        @pl.when(me == r)
        def _():
            ssum[0:1, r * cols : (r + 1) * cols] = sq[0:1]
            ssum[1:2, r * cols : (r + 1) * cols] = sv[0:1]

    send1 = [across_mp(j, ssum, slot1.at[j], s1s.at[j], s1r.at[j]) for j in range(1, n_mp)]
    for c in send1:
        c.start()

    total = jnp.zeros((xt.shape[0], 3 * cols), F32)
    for c in range(n_mp):
        total += dot_nt(xt[:, c * own : (c + 1) * own], dbuf[c].reshape(3 * cols, own))
    for d in range(n_dp):
        gbuf[d] = total[d * wrows : (d + 1) * wrows].astype(BF)

    def weight_copy(j):
        to = lax.rem(me_dp + j, n_dp)
        return across_dp(j, gbuf.at[to], qland.at[j], ws_sem.at[j], wr_sem.at[j])

    for j in range(1, n_dp):
        weight_copy(j).start()

    add_cross(1)
    for c in send1:
        c.wait_send()
        c.wait_recv()
    total = ssum[...]
    for j in range(1, n_mp):
        total += slot1[j]
    ssum[...] = total
    send2 = [across_dp(j, ssum, slot2.at[j], s2s.at[j], s2r.at[j]) for j in range(1, n_dp)]
    for c in send2:
        c.start()

    fetch_w.wait()
    into = dot(wfull[me, :, : 3 * cols], dbuf[me].reshape(3 * cols, own))
    for j in range(1, n_mp):
        for h in range(heads):
            query_copy(h, j).wait_recv()
            pair_copy(h, j).wait_recv()
        r = lax.rem(me + j, n_mp)
        into += dot(wfull[r, :, : 3 * cols], dland[j].reshape(3 * cols, own))
    grad_in[...] = (dsum1[...] + into.T).astype(BF)

    for o in range(2, n_mp):
        add_cross(o)
    total = gbuf[me_dp].astype(F32)
    for j in range(1, n_dp):
        weight_copy(j).wait_recv()
        total += qland[j].astype(F32)
    gq[...] = total
    total = ssum[...]
    for c in send2:
        c.wait_recv()
    for j in range(1, n_dp):
        total += slot2[j]
    small[...] = total
    for t, out in ((0, gff), (1, gout)):
        total, land = kinds[t][4:]
        for o in range(n_mp - 1):
            along(o, t).wait_recv()
        for m in range(out.shape[0]):
            a = total[n_mp - 1, m].astype(F32)
            for o in range(n_mp - 1):
                a += land[o, m].astype(F32)
            out[m] = a
    for t in range(2):
        for o in range(n_mp):
            pair_up(o, t).wait_send()
            for j in range(1, n_q):
                cross(o, j, t).wait_send()
            if o < n_mp - 1:
                along(o, t).wait_send()
    for c in send2:
        c.wait_send()
    for j in range(1, n_dp):
        weight_copy(j).wait_send()
    for h in range(heads):
        for j in range(1, n_mp):
            grad_copy(h, j).wait_send()
            query_copy(h, j).wait_send()
            pair_copy(h, j).wait_send()


def norm_parts(r):
    centre = r - jnp.mean(r, axis=-1, keepdims=True)
    spread = jnp.mean(centre * centre, axis=-1, keepdims=True)
    rstd = lax.rsqrt(spread + 1e-05)
    return centre * rstd, rstd


def norm_back(dn, n, rstd):
    return rstd * (
        dn - jnp.mean(dn, axis=-1, keepdims=True) - n * jnp.mean(dn * n, axis=-1, keepdims=True)
    )


def colsum(a):
    return jnp.sum(a, axis=0, keepdims=True)


def flip(a):
    return a.astype(F32).T.astype(BF)


GELU_C = 0.7978845608
GELU_A = 0.044715


def middle(
    attn, x, cot, wlast, small, w,
    result, dsum1, dattn, gw, gwout, gsmall,
    wout, mid, midb, midt, gate, up, y, dffn, dffnt, dmid,
):
    i = pl.program_id(0)
    n = pl.num_programs(0) // 2
    parts, cols = attn.shape[0], attn.shape[1]

    @pl.when(i == 0)
    def _():
        branch = jnp.zeros((x.shape[1], x.shape[0]), F32)
        for r in range(parts):
            wout[r] = wlast[0, r, :, 3 * cols :]
            branch += dot(wout[r], attn[r])
        branch = branch.T + x[...].astype(F32) + small[2:3, :]
        nn, _ = norm_parts(branch)
        m = nn * small[3:4, :] + small[4:5, :]
        dsum1[...] = branch
        mid[...] = m
        midb[...] = m.astype(BF)
        midt[...] = m.T.astype(BF)
        y[...] = jnp.zeros_like(y)

    @pl.when(i < n)
    def _():
        mb = midb[...]
        ga = dot(mb, w[0, 0]) + small[pl.ds(8 + i, 1), :]
        u = dot(mb, w[1, 0]) + small[pl.ds(8 + n + i, 1), :]
        gate[i] = ga
        up[i] = u
        t = jnp.tanh(GELU_C * (ga + GELU_A * ga * ga * ga))
        act = (0.5 * ga * (1.0 + t) * u).astype(BF)
        y[...] += dot_nt(act, w[2, 0])

    @pl.when(i == n - 1)
    def _():
        r = mid[...] + y[...] + small[5:6, :]
        nn, rstd = norm_parts(r)
        gain = small[6:7, :]
        result[...] = (nn * gain + small[7:8, :]).astype(BF)
        c = cot[...].astype(F32)
        ds = norm_back(c * gain, nn, rstd)
        gsmall[6:7, :] = colsum(c * nn)
        gsmall[7:8, :] = colsum(c)
        dmid[...] = ds
        db = ds.astype(BF)
        dffn[...] = db
        dffnt[...] = ds.T.astype(BF)
        gsmall[5:6, :] = colsum(db.astype(F32))
        gsmall[0:2, :] = jnp.zeros_like(gsmall[0:2, :])

    @pl.when(i >= n)
    def _():
        k = 2 * n - 1 - i
        ga = gate[k]
        u = up[k]
        sq = ga * ga
        t = jnp.tanh(GELU_C * (ga + GELU_A * ga * sq))
        half = 0.5 * (1.0 + t)
        gelu = ga * half
        slope = half + (0.5 * GELU_C) * ga * (1.0 - t * t) * (1.0 + 3.0 * GELU_A * sq)
        act = (gelu * u).astype(BF)
        dact = dot(dffn[...], w[2, 0])
        gw[0, 2] = dot(dffnt[...], act).astype(BF)
        dga = (dact * u * slope).astype(BF)
        du = (dact * gelu).astype(BF)
        gsmall[pl.ds(8 + k, 1), :] = colsum(dga.astype(F32))
        gsmall[pl.ds(8 + n + k, 1), :] = colsum(du.astype(F32))
        gw[0, 0] = dot(midt[...], dga).astype(BF)
        gw[0, 1] = dot(midt[...], du).astype(BF)
        dmid[...] += dot_nt(dga, w[0, 0]) + dot_nt(du, w[1, 0])

    @pl.when(i == 2 * n - 1)
    def _():
        nn, rstd = norm_parts(dsum1[...])
        dm = dmid[...]
        gsmall[3:4, :] = colsum(dm * nn)
        gsmall[4:5, :] = colsum(dm)
        ds = norm_back(dm * small[3:4, :], nn, rstd)
        dsum1[...] = ds
        db = ds.astype(BF)
        gsmall[2:3, :] = colsum(db.astype(F32))
        dbt = ds.T.astype(BF)
        for r in range(parts):
            dattn[r] = dot(db, wout[r]).T.astype(BF)
            gwout[r] = dot_nt(dbt, attn[r]).astype(BF)


def head_slopes(first_head, head_count):
    number = first_head + jnp.arange(head_count, dtype=jnp.int32)
    exponent = jnp.where(number < 8, number.astype(F32) + 1.0, number.astype(F32) - 7.5)
    return jnp.exp2(-exponent)


def cost(flops):
    return pl.CostEstimate(flops=flops, bytes_accessed=1 << 24, transcendentals=0)


def params(**kw):
    return pltpu.CompilerParams(vmem_limit_bytes=VMEM_LIMIT, **kw)


def per_device(
    hidden_in, lengths, w_qkv, b_qv, w_out, b_out, ln1_gain, ln1_bias, w_gu, b_gu, w_down,
    b_down, ln2_gain, ln2_bias, cotangent,
):
    both = ("dp", "mp")
    n_dp, n_mp = lax.axis_size("dp"), lax.axis_size("mp")
    n = n_dp * n_mp
    mp_rank = lax.axis_index("mp")
    own, width = hidden_in.shape
    group = own * n_mp
    sds = jax.ShapeDtypeStruct

    dev = lax.axis_index("dp") * n_mp + mp_rank

    def placed(a):
        zero = jnp.zeros((a.shape[0], a.shape[1] * n), F32)
        return lax.dynamic_update_slice_in_dim(zero, a, dev * a.shape[1], 1)

    vectors = jnp.stack([b_out, ln1_gain, ln1_bias, b_down, ln2_gain, ln2_bias])
    vectors = jnp.concatenate([b_qv, vectors], axis=0)
    small_own = jnp.concatenate(
        [placed(vectors), placed(b_gu).reshape(-1, width)], axis=0
    )
    srows = small_own.shape[0]

    wq = w_qkv.astype(BF)
    wrows, cols = wq.shape[1], wq.shape[2]
    ff_part = w_gu.shape[2]
    heads = cols // HEAD
    tail = group - LONGEST

    attn_pack = jnp.concatenate([wq[0], wq[1], wq[2], w_out.T.astype(BF)], axis=1)
    pack = jnp.concatenate([w_gu.astype(BF), w_down.T.astype(BF)[None], attn_pack[None]], axis=0)
    weights = lax.all_gather(pack, ("mp", "dp"), axis=1, tiled=True)
    weights = weights.reshape(4, n_mp, width, ff_part)

    slopes = head_slopes(mp_rank * heads, heads)
    dma = pltpu.SemaphoreType.DMA

    small, xt, qt, kp, vte, ut, attn, p, p2 = pl.pallas_call(
        functools.partial(front, n_dp, n_mp),
        out_shape=(
            sds((srows, width), F32),
            sds((width, group), BF),
            sds((cols, group), BF),
            sds((heads, group, 2 * HEAD), BF),
            sds((heads, 2 * HEAD, group), BF),
            sds((heads, 2 * HEAD, group), F32),
            sds((n_mp, cols, own), BF),
            sds((heads, LONGEST, LONGEST), BF),
            sds((heads, tail, tail), BF),
        ),
        in_specs=[vmem(), vmem(), vmem(), smem(), smem()],
        out_specs=(vmem(), vmem(), vmem(), vmem(), vmem(), vmem(), vmem(), hbm(), vmem()),
        scratch_shapes=[
            pltpu.VMEM((n_mp, own, width), BF),
            pltpu.VMEM((n_dp, 3, wrows, cols), BF),
            pltpu.VMEM((3, width, cols), F32),
            pltpu.VMEM((3, width, cols), BF),
            pltpu.VMEM((n_mp, srows, width), F32),
            pltpu.VMEM((srows, width), F32),
            pltpu.VMEM((n_dp, srows, width), F32),
            pltpu.VMEM((8, cols), F32),
            pltpu.VMEM((group, cols), BF),
            pltpu.VMEM((cols, group), BF),
            pltpu.VMEM((heads, group, 2 * HEAD), BF),
            pltpu.VMEM((QB, LONGEST + LONGEST // QB * QB), F32),
            pltpu.VMEM((heads, LONGEST, LONGEST), BF),
            pltpu.VMEM((n_mp, cols, own), BF),
            pltpu.VMEM((n_mp, cols, own), BF),
            dma((2, n_mp - 1, PIECES)),
            dma((2, n_mp - 1, PIECES)),
            dma((n_dp,)),
            dma((n_dp,)),
            dma((n_mp,)),
            dma((n_mp,)),
            dma((n_dp,)),
            dma((n_dp,)),
            dma((heads, n_mp)),
            dma((heads, n_mp)),
            dma((heads,)),
        ],
        compiler_params=params(collective_id=0, has_side_effects=True),
        cost_estimate=cost(11 * LONGEST * LONGEST * HEAD * heads * 12),
        name="front",
    )(hidden_in, wq, small_own, slopes, lengths)

    fixed = lambda *s: pl.BlockSpec(s, lambda i: (0,) * len(s))
    walk = lambda i: jnp.where(i < n_mp, i, 2 * n_mp - 1 - i)
    late = lambda i: jnp.where(i < n_mp, n_mp - 1, 2 * n_mp - 1 - i)
    result, dsum1, dattn, gw, gwout, gsmall = pl.pallas_call(
        middle,
        grid=(2 * n_mp,),
        out_shape=(
            sds((own, width), BF),
            sds((own, width), F32),
            sds((n_mp, cols, own), BF),
            sds((n_mp, 3, width, ff_part), BF),
            sds((n_mp, width, cols), BF),
            sds((srows, width), F32),
        ),
        in_specs=[
            fixed(n_mp, cols, own),
            fixed(own, width),
            fixed(own, width),
            pl.BlockSpec(
                (1, n_mp, width, ff_part),
                lambda i: (3, 0, 0, 0),
                pipeline_mode=pl.Buffered(1),
            ),
            fixed(srows, width),
            pl.BlockSpec((3, 1, width, ff_part), lambda i: (0, walk(i), 0, 0)),
        ],
        out_specs=(
            fixed(own, width),
            fixed(own, width),
            fixed(n_mp, cols, own),
            pl.BlockSpec((1, 3, width, ff_part), lambda i: (late(i), 0, 0, 0)),
            fixed(n_mp, width, cols),
            fixed(srows, width),
        ),
        scratch_shapes=[
            pltpu.VMEM((n_mp, width, cols), BF),
            pltpu.VMEM((own, width), F32),
            pltpu.VMEM((own, width), BF),
            pltpu.VMEM((width, own), BF),
            pltpu.VMEM((n_mp, own, ff_part), F32),
            pltpu.VMEM((n_mp, own, ff_part), F32),
            pltpu.VMEM((own, width), F32),
            pltpu.VMEM((own, width), BF),
            pltpu.VMEM((width, own), BF),
            pltpu.VMEM((own, width), F32),
        ],
        compiler_params=params(),
        name="middle",
    )(attn, hidden_in, cotangent, weights, small, weights)

    n_q = n_dp // 2
    gw = gw.reshape(n_mp, 3, n_q, 2, wrows, ff_part)
    gwout = gwout.reshape(n_mp, 1, n_q, 2, wrows, cols)
    grad_in, gqkv, gsmall, gff, gout = pl.pallas_call(
        functools.partial(back, n_dp, n_mp),
        out_shape=(
            sds((own, width), BF),
            sds((wrows, 3 * cols), F32),
            sds((srows, width), F32),
            sds((3, wrows, ff_part), F32),
            sds((1, wrows, cols), F32),
        ),
        in_specs=[
            vmem(), vmem(), vmem(), vmem(), vmem(), vmem(), hbm(), vmem(), hbm(), vmem(), vmem(),
            hbm(), hbm(),
        ],
        out_specs=(vmem(), vmem(), vmem(), vmem(), vmem()),
        scratch_shapes=[
            pltpu.VMEM((n_mp, cols, own), BF),
            pltpu.VMEM((2, own, LONGEST), BF),
            pltpu.VMEM((HEAD, group), F32),
            pltpu.VMEM((HEAD, group), F32),
            pltpu.VMEM((n_mp, 3, cols, own), BF),
            pltpu.VMEM((n_mp, 3, cols, own), BF),
            pltpu.VMEM((n_mp, width, ff_part), BF),
            pltpu.VMEM((n_dp, wrows, 3 * cols), BF),
            pltpu.VMEM((n_dp, wrows, 3 * cols), BF),
            pltpu.VMEM((srows, width), F32),
            pltpu.VMEM((n_mp, srows, width), F32),
            pltpu.VMEM((n_dp, srows, width), F32),
            pltpu.VMEM((n_mp, 3, n_q, wrows, ff_part), BF),
            pltpu.VMEM((n_mp, 3, n_q, wrows, ff_part), BF),
            pltpu.VMEM((n_mp, n_q - 1, 3, wrows, ff_part), BF),
            pltpu.VMEM((n_mp, 3, wrows, ff_part), BF),
            pltpu.VMEM((n_mp - 1, 3, wrows, ff_part), BF),
            pltpu.VMEM((n_mp, 1, n_q, wrows, cols), BF),
            pltpu.VMEM((n_mp, 1, n_q, wrows, cols), BF),
            pltpu.VMEM((n_mp, n_q - 1, 1, wrows, cols), BF),
            pltpu.VMEM((n_mp, 1, wrows, cols), BF),
            pltpu.VMEM((n_mp - 1, 1, wrows, cols), BF),
            dma((heads, n_mp)),
            dma((heads, n_mp)),
            dma((heads, n_mp)),
            dma((heads, n_mp)),
            dma((heads, n_mp)),
            dma((heads, n_mp)),
            dma((n_dp,)),
            dma((n_dp,)),
            dma((n_mp,)),
            dma((n_mp,)),
            dma((n_dp,)),
            dma((n_dp,)),
            dma((2,)),
            dma,
            dma((n_mp, 2)),
            dma((n_mp, 2)),
            dma((n_mp, 2)),
            dma((n_mp, n_q, 2)),
            dma((n_mp, n_q, 2)),
            dma((n_mp - 1, 2)),
            dma((n_mp - 1, 2)),
        ],
        compiler_params=params(collective_id=1, has_side_effects=True),
        cost_estimate=cost(11 * LONGEST * LONGEST * HEAD * heads * 12),
        name="back",
    )(dattn, xt, qt, kp, vte, ut, p, p2, weights, dsum1, gsmall, gw, gwout)

    def own_columns(a):
        part = a.shape[1] // n
        return lax.dynamic_slice_in_dim(a, dev * part, part, 1)

    gs = own_columns(gsmall[:8])
    g_gu = own_columns(gsmall[8:].reshape(2, -1))
    gqkv = gqkv.reshape(wrows, 3, cols).transpose(1, 0, 2)

    return (
        result,
        grad_in,
        gqkv,
        gs[0:2],
        gout[0].T,
        gs[2],
        gs[3],
        gs[4],
        gff[:2],
        g_gu,
        gff[2].T,
        gs[5],
        gs[6],
        gs[7],
    )


def solution(mesh):
    rows = P(("dp", "mp"), None)
    vec = P(("dp", "mp"))
    vecs = P(None, ("dp", "mp"))
    wide = P(None, "dp", "mp")
    tall = P("mp", "dp")
    return jax.shard_map(
        per_device,
        mesh=mesh,
        in_specs=(
            rows, P("dp", None), wide, vecs, tall, vec, vec, vec, wide, vecs, tall, vec, vec, vec,
            rows,
        ),
        out_specs=(
            rows, rows, wide, vecs, tall, vec, vec, vec, wide, vecs, tall, vec, vec, vec,
        ),
        check_vma=False,
    )
```

time: 531 us -> 370 us (0.70)
  Pallas kernels: 110 us -> 319 us
  waiting for transfers between devices: 166 us -> 13.6 us
  blocking collectives: 148 us -> 0 us
  local copies, waits for them, and re-layouts: 53.3 us -> 12.3 us
  matrix products: 10.6 us -> 0 us
  starting transfers between devices: 8.28 us -> 0.04 us
    pallas_call x2, Pallas kernels: 70.1 us -> 278 us  [the longest x1 152 us: per_device(): pl.pallas_call(functools.partial(front, n_dp, n_mp), out_shape=(sds((srow...]
    reduce_scatter x4 -> x0, waiting for transfers between devices: 90.1 us -> none  [the longest x1 57.1 us: per_device(): gw = lax.psum_scatter(gw, 'dp', scatter_dimension=2, tiled=True)]
    all_gather x2 -> x0, blocking collectives: 85.5 us -> none  [the longest x1 71.9 us: per_device(): small_all = lax.all_gather(small_flat, both, axis=0, tiled=True)]
    unnamed x1 -> x0, blocking collectives: 39.7 us -> none
    all_to_all x2 -> x0, waiting for transfers between devices: 39.5 us -> none  [the longest x1 39.5 us: per_device(): attn = lax.all_to_all(o, 'mp', 0, 0, tiled=True)]
    all_to_all x1 -> x0, blocking collectives: 23.2 us -> none  [per_device(): g = lax.all_to_all(dattn, 'mp', 0, 0, tiled=True)]
    slice x13 -> x2, local copies, waits for them, and re-layouts: 25 us -> 2.75 us  [the longest x1 1.92 us: per_device(): gff[:2]]
    all_gather x1, waiting for transfers between devices: 32 us -> 13.5 us  [per_device(): weights = lax.all_gather(pack, ('mp', 'dp'), axis=1, tiled=True)]
  transfers between devices with their start and end apart: 9 -> 1, of which waited for: 5 -> 1; matrix products, arithmetic and copies ran while one was open for 10% -> 0% of each run, Pallas kernels for 13% -> 42%
where the time goes in v2:
time: 370 us; the launch traced here: 365 us
  Pallas kernels  319 us (86%)
  between operations  14.6 us (4%)
  waiting for transfers between devices  13.6 us (4%)
  local copies, waits for them, and re-layouts  12.3 us (3%)
  other arithmetic  5.2 us (1%)
    pallas_call x1, Pallas kernels, per_device(): pl.pallas_call(functools.partial(front, n_dp, n_mp), out_shape=(sds((srow...  152 us
    pallas_call x1, Pallas kernels, per_device(): pl.pallas_call(functools.partial(back, n_dp, n_mp), out_shape=(sds((own,...  126 us
    pallas_call x1, Pallas kernels, per_device(): pl.pallas_call(middle, grid=(2 * n_mp,), out_shape=(sds((own, width), BF)...  40.9 us
    all_gather x1, waiting for transfers between devices, per_device(): weights = lax.all_gather(pack, ('mp', 'dp'), axis=1, tiled=True)  13.5 us
  transfers between devices with their start and end apart: 1, of which 1 were waited for; matrix products, arithmetic and copies ran while one was open for 0% of the time, Pallas kernels for 42%

profile of v2, /device:TPU:0, one launch (start us, length us, event | category | flops | bytes accessed | tf_op | source)
XLA Modules:
  0.0 364.6 jit_solution(16919853081776602258)
XLA Ops:
  7.2 0.0 copy-start.2
  7.2 0.0 copy-start.3
  7.2 0.0 copy-start.4
  7.2 0.0 copy-start.5
  7.2 0.0 copy-start.6
  7.2 0.0 copy-start.7
  7.2 0.0 copy-start.8
  7.3 0.0 copy-start.9
  7.3 0.0 all-gather.2.cloned.1.call-start
  7.3 1.0 convert_element_type.22.wq
  8.3 0.0 copy-start.1
  8.3 1.0 copy.32
  9.4 1.0 convert_bitcast_fusion
  10.4 1.1 convert_element_type.24
  11.5 0.1 maximum_bitcast_fusion
  11.6 0.9 pad_maximum_fusion
  12.4 0.0 all-gather.2.cloned.1.call-update
  12.5 0.0 copy-done.2
  12.5 0.2 dynamic_update_slice.7
  12.7 0.0 copy-done.3
  12.7 0.0 copy-done.4
  12.7 0.0 copy-done.5
  12.7 0.0 copy-done.6
  12.7 0.0 copy-done.7
  12.8 0.0 copy-done.8
  12.8 0.0 copy-done.9
  12.8 0.3 dynamic_update_slice.6
  13.1 0.5 multiply_exponential_fusion.slope
  13.6 0.6 pad_maximum_fusion.1.sin
  14.2 0.0 copy-done.1
  14.2 152.1 %front.1 = (f32[16,768]{1,0:T(8,128)}, bf16[768,2048]{1,0:T(8,128)(2,1)}, bf16[192,2048]{1,0:T(8,128)(2,1)}, bf16[3,2048,128]{2,1,0:T(8,128)(2,1)}, bf16[3,128,2...) custom-call(bf16[512,768]{1,0:T(8,128)(2,1)} %x.3, ...), custom_call_target="tpu_custom_call" | custom-call | flops 70174900224 | bytes 16777216 | tf_op jit(solution)/shard_map/front/pallas_call | solution.py:808
  166.4 13.5 %all-gather.2.cloned.1.call-done = bf16[4,3072,768]{2,1,0:T(8,128)(2,1)} async-done(((bf16[4,96,768]{2,1,0:T(8,128)(2,1)}), bf16[4,3072,768]{2,1,0:T(8,128)(2,1)}) %all-gather.2.cloned.1.call-update) | async-done | bytes 18874384 | tf_op jit(solution)/shard_map/all_gather | solution.py:802
  179.9 40.9 %middle.1 = (bf16[512,768]{1,0:T(8,128)(2,1)}, f32[512,768]{1,0:T(8,128)}, bf16[4,192,512]{2,1,0:T(8,128)(2,1)}, bf16[4,3,768,768]{3,2,1,0:T(8,128)(2,1)}, bf16[...) custom-call(bf16[4,192,512]{2,1,0:T(8,128)(2,1)} %get-tuple-element.34.attn, bf16[512,768]{1,0:T(8,128)(2,1)} %x.3, ...), custom_call_target="tpu_custom_call" | custom-call | tf_op jit(solution)/shard_map/middle/pallas_call | solution.py:859
  220.8 125.9 %back.1 = (bf16[512,768]{1,0:T(8,128)(2,1)}, f32[96,576]{1,0:T(8,128)}, f32[16,768]{1,0:T(8,128)}, f32[3,96,768]{2,1,0:T(8,128)}, f32[1,96,192]{2,1,0:T(8,128)}) custom-call(bf16[4,192,512]{2,1,0:T(8,128)(2,1)} %get-tuple-element.37.gt, bf16[768,2048]{1,0:T(8,128)(2,1)} %get-tuple-element.38.xt, bf16[192,2048]{1,0:T(8,128)(2,1)} %get-tuple-element.39.qt, ...), custom_call_target="tpu_custom_call" | custom-call | flops 70174900224 | bytes 16777216 | tf_op jit(solution)/shard_map/back/pallas_call | solution.py:909
  346.7 0.0 copy-start
  346.7 0.8 fusion.1
  347.6 0.1 constant_dynamic-slice_fusion.1
  347.6 0.6 slice.46
  348.2 0.5 slice_bitcast_fusion.4
  348.7 1.9 slice.50
  350.7 1.7 slice_bitcast_fusion
  352.4 1.1 copy.33
  353.4 0.9 copy.34
  354.3 1.6 copy.35
  356.0 0.6 constant_dynamic-slice_fusion
  356.6 0.0 copy-done
  356.6 0.9 copy.39
  (6 shorter events, 0.1 us)
Async XLA Ops:
  7.2 5.3 %copy-start.2 = (f32[2,96]{1,0:T(2,128)S(1)}, f32[2,96]{1,0:T(2,128)}, u32[]{:S(2)}) copy-start(f32[2,96]{1,0:T(2,128)} %param.24) | copy-start | bytes 2308
  7.2 5.5 %copy-start.3 = (f32[2,24]{1,0:T(2,128)S(1)}, f32[2,24]{1,0:T(2,128)}, u32[]{:S(2)}) copy-start(f32[2,24]{1,0:T(2,128)} %param.18) | copy-start | bytes 580
  7.2 5.5 %copy-start.4 = (f32[24]{0:T(128)S(1)}, f32[24]{0:T(128)}, u32[]{:S(2)}) copy-start(f32[24]{0:T(128)} %param.20) | copy-start | bytes 292
  7.2 5.5 %copy-start.5 = (f32[24]{0:T(128)S(1)}, f32[24]{0:T(128)}, u32[]{:S(2)}) copy-start(f32[24]{0:T(128)} %param.21) | copy-start | bytes 292
  7.2 5.5 %copy-start.6 = (f32[24]{0:T(128)S(1)}, f32[24]{0:T(128)}, u32[]{:S(2)}) copy-start(f32[24]{0:T(128)} %param.22) | copy-start | bytes 292
  7.2 5.5 %copy-start.7 = (f32[24]{0:T(128)S(1)}, f32[24]{0:T(128)}, u32[]{:S(2)}) copy-start(f32[24]{0:T(128)} %param.26) | copy-start | bytes 292
  7.2 5.5 %copy-start.8 = (f32[24]{0:T(128)S(1)}, f32[24]{0:T(128)}, u32[]{:S(2)}) copy-start(f32[24]{0:T(128)} %param.27) | copy-start | bytes 292
  7.3 5.5 %copy-start.9 = (f32[24]{0:T(128)S(1)}, f32[24]{0:T(128)}, u32[]{:S(2)}) copy-start(f32[24]{0:T(128)} %param.28) | copy-start | bytes 292
  7.3 172.7 %all-gather.2.cloned.1.call-start = ((), (), s32[]{:S(2)}) async-start(), calls=%async_computation | async-start | bytes 19464192 | tf_op jit(solution)/shard_map/all_gather | solution.py:802
  8.3 5.9 %copy-start.1 = (bf16[3,96,192]{2,1,0:T(8,128)(2,1)}, bf16[3,96,192]{2,1,0:T(8,128)(2,1)S(1)}, u32[]{:S(2)}) copy-start(bf16[3,96,192]{2,1,0:T(8,128)(2,1)S(1)} %convert_element_type.22.wq) | copy-start | bytes 331780
  346.7 9.9 %copy-start = (bf16[512,768]{1,0:T(8,128)(2,1)S(1)}, bf16[512,768]{1,0:T(8,128)(2,1)}, u32[]{:S(2)}) copy-start(bf16[512,768]{1,0:T(8,128)(2,1)} %get-tuple-element.108) | copy-start | bytes 2359300
Sparse Core Ops, SparseCore 0:
  12.6 167.2 all-gather.1

commit v3 on v2

--- a/solution.py
+++ b/solution.py
@@ -54,15 +54,16 @@
 
 def front(
     n_dp, n_mp,
-    x, wq, sin, slope, length,
-    small, xt, qt, kp, vte, ut, attnt, p, p2,
-    hid, wslot, wf, wb, slot1, ssum, slot2, bias, qs, kt, vext, dist, pbuf, obuf, land,
-    hs_sem, hr_sem, ws_sem, wr_sem, s1s, s1r, s2s, s2r, os_sem, or_sem, psem,
+    x, pack, sin, slope, length,
+    small, xt_out, qt_out, kp_out, vte_out, ut_out, attnt, p, p2_out, wall,
+    xt, qt, kp, vte, ut, p2, hid, wslot, wf, wb, slot1, ssum, slot2, bias, qs, kt, vext, dist, pbuf, obuf, land,
+    hs_sem, hr_sem, s1s, s1r, s2s, s2r, os_sem, or_sem, psem,
+    local_sem, early_sem, late_sem, wzs, wzr, wqs, wqr, wps, wpr,
 ):
     me_dp, me = lax.axis_index("dp"), lax.axis_index("mp")
     own = x.shape[0]
     group = own * n_mp
-    wrows, cols = wq.shape[1], wq.shape[2]
+    wrows, cols = pack.shape[1], wb.shape[2]
     heads = cols // HEAD
     tail = group - LONGEST
     full = LONGEST // own
@@ -86,9 +87,8 @@
     greet(n_dp, n_mp, me_dp, me)
 
     send1 = [across_mp(j, sin, slot1.at[j], s1s.at[j], s1r.at[j]) for j in range(1, n_mp)]
-    sendw = [across_dp(j, wq, wslot.at[j], ws_sem.at[j], wr_sem.at[j]) for j in range(1, n_dp)]
     send2 = [across_dp(j, ssum, slot2.at[j], s2s.at[j], s2r.at[j]) for j in range(1, n_dp)]
-    for c in send1 + sendw:
+    for c in send1:
         c.start()
 
     def hidden(way, step, k):
@@ -125,8 +125,126 @@
             def _():
                 hidden(way, step, k).wait_recv()
 
+    n_q = n_dp // 2
+    me_q, me_c = me_dp // 2, lax.rem(me_dp, 2)
+    square = n_q == 4
+    halves = ((3, 2), (0, 1))
+
+    def unit_rank(level):
+        if level == 0:
+            return me
+        step, way = (level - 1) // 2, (level - 1) % 2
+        return jnp.clip(me - 1 - step if way == 0 else me + 1 + step, 0, n_mp - 1)
+
+    def here(level):
+        return True if level == 0 else receives((level - 1) % 2, (level - 1) // 2)
+
+    def mate(j):
+        if not square:
+            return lax.rem(me_q + j, n_q)
+        x1, y1 = lax.rem(me_q, 2), me_q // 2
+        x2 = 1 - x1 if j % 2 else x1
+        y2 = 1 - y1 if j // 2 else y1
+        return 2 * y2 + x2
+
+    def weight_z(way, step, m):
+        level = 0 if step == 0 else 1 + 2 * (step - 1) + way
+        r = unit_rank(level)
+        to = jnp.clip(me + 1 if way == 0 else me - 1, 0, n_mp - 1)
+        dst = wall.at[m, r, me_q, me_c]
+        src = pack.at[m] if step == 0 else dst
+        return pltpu.make_async_remote_copy(
+            src_ref=src, dst_ref=dst,
+            send_sem=wzs.at[way, step, m], recv_sem=wzr.at[way, step, m],
+            device_id=(me_dp, to), device_id_type=MESH,
+        )
+
+    def weight_q(level, m, slot):
+        r = unit_rank(level)
+        j, what = (slot, 0) if slot else ((1, 2) if m % 2 else (2, 1))
+        dst = wall.at[m, r, mate(what), me_c]
+        src = pack.at[m] if level == 0 and slot else dst
+        return pltpu.make_async_remote_copy(
+            src_ref=src, dst_ref=dst,
+            send_sem=wqs.at[level, m, slot], recv_sem=wqr.at[level, m, slot],
+            device_id=(mate(j) * 2 + me_c, me), device_id_type=MESH,
+        )
+
+    def weight_p(level, half, j):
+        part = pl.ds(min(halves[half]), 2)
+        dst = wall.at[part, unit_rank(level), mate(j), me_c]
+        src = pack.at[part] if level == 0 and j == 0 else dst
+        return pltpu.make_async_remote_copy(
+            src_ref=src, dst_ref=dst,
+            send_sem=wps.at[level, half, j], recv_sem=wpr.at[level, half, j],
+            device_id=(me_q * 2 + 1 - me_c, me), device_id_type=MESH,
+        )
+
+    near = (1, 2) if square else tuple(range(1, n_q))
+    slots = ((0,) if square else ()) + near
+
+    def weight_on(way, step, m):
+        @pl.when(sends(way, step))
+        def _():
+            weight_z(way, step, m).start()
+
+    def weight_stage(level, stage, half):
+        step, way = (level - 1) // 2, (level - 1) % 2
+
+        def run():
+            for m in halves[half]:
+                if stage == 0:
+                    if level > 0:
+                        weight_z(way, step, m).wait_recv()
+                        if 0 < step < n_mp - 2:
+                            weight_on(way, step + 1, m)
+                    for j in near:
+                        weight_q(level, m, j).start()
+                elif stage == 1:
+                    if square:
+                        weight_q(level, m, 2 if m % 2 else 1).wait_recv()
+                        weight_q(level, m, 0).start()
+                        weight_q(level, m, 1 if m % 2 else 2).wait_recv()
+                    else:
+                        for j in near:
+                            weight_q(level, m, j).wait_recv()
+                elif stage == 2 and square:
+                    weight_q(level, m, 0).wait_recv()
+                elif stage == 4:
+                    for j in slots:
+                        weight_q(level, m, j).wait_send()
+            if stage == 0:
+                weight_p(level, half, 0).start()
+            elif stage == 1:
+                for j in near:
+                    weight_p(level, half, j).start()
+            elif stage == 2 and square:
+                weight_p(level, half, 3).start()
+            elif stage == 3:
+                for j in range(n_q):
+                    weight_p(level, half, j).wait_recv()
+            elif stage == 4:
+                for j in range(n_q):
+                    weight_p(level, half, j).wait_send()
+
+        if level == 0:
+            run()
+        else:
+            pl.when(here(level))(run)
+
+    def both_ways(step, stage, half):
+        for way in range(2):
+            weight_stage(1 + 2 * step + way, stage, half)
+
     for k in range(PIECES):
         send_hidden(0, k)
+    for half in range(2):
+        for m in halves[half]:
+            for way in range(2):
+                weight_on(way, 0, m)
+        weight_stage(0, 0, half)
+    keep = pltpu.make_async_copy(pack, wall.at[:, me, me_q, me_c], local_sem.at[0])
+    keep.start()
 
     width = dist.shape[1]
     base = width - LONGEST
@@ -145,18 +263,15 @@
 
     for k in range(PIECES):
         wait_hidden(0, k)
-        if n_mp > 2:
-            send_hidden(1, k)
-
-    for c in sendw:
-        c.wait_recv()
-    for j in range(n_dp):
-        place = pl.multiple_of(lax.rem(me_dp - j + n_dp, n_dp) * wrows, wrows)
-        for s in range(3):
-            part = wq[s] if j == 0 else wslot[j, s]
-            wf[s, pl.ds(place, wrows), :] = part.astype(F32)
-    for s in range(3):
-        wb[s] = wf[s].astype(BF)
+        send_hidden(1, k)
+
+    for stage in range(1, 4):
+        weight_stage(0, stage, 0)
+        if stage == 1:
+            weight_stage(0, 1, 1)
+    keep.wait()
+    fetch = pltpu.make_async_copy(wall.at[3, me], wslot, local_sem.at[1])
+    fetch.start()
 
     for c in send2:
         c.wait_recv()
@@ -170,6 +285,14 @@
         @pl.when(me == r)
         def _():
             bias[0:2, :] = total[0:2, r * cols : (r + 1) * cols]
+
+    fetch.wait()
+    for j in range(n_dp):
+        for s in range(3):
+            part = wslot[j // 2, j % 2, :, s * cols : (s + 1) * cols]
+            wf[s, j * wrows : (j + 1) * wrows, :] = part.astype(F32)
+    for s in range(3):
+        wb[s] = wf[s].astype(BF)
 
     one = jnp.where(lax.broadcasted_iota(jnp.int32, (QB, HEAD), 1) == 0, 1.0, 0.0)
     minus = jnp.where(lax.broadcasted_iota(jnp.int32, (HEAD, QB), 0) < 2, -1.0, 0.0)
@@ -198,19 +321,45 @@
         lax.fori_loop(0, own // QB, part, 0)
 
     project(x, me)
-    for step in range(1, n_mp):
-        if step > 1:
+    for half in range(2):
+        both_ways(0, 0, half)
+    for step in range(n_mp - 1):
+        if step > 0:
             for k in range(PIECES):
-                wait_hidden(step - 1, k)
-                if step < n_mp - 1:
-                    send_hidden(step, k)
+                wait_hidden(step, k)
+                if step < n_mp - 2:
+                    send_hidden(step + 1, k)
+        if step == n_mp - 2:
+            for way in range(2):
+
+                @pl.when(sends(way, step))
+                def _():
+                    for k in range(PIECES):
+                        hidden(way, step, k).wait_send()
+
+                for half in range(2):
+                    for m in halves[half]:
+                        weight_on(way, 1, m)
+
         for way in range(2):
 
-            @pl.when(receives(way, step - 1))
+            @pl.when(receives(way, step))
             def _():
-                shard = me - step if way == 0 else me + step
+                shard = me - 1 - step if way == 0 else me + 1 + step
                 shard = jnp.clip(shard, 0, n_mp - 1)
                 project(hid.at[shard], shard)
+
+        if step == 1:
+            weight_stage(0, 2, 1)
+            for half in range(2):
+                both_ways(0, 1, half)
+
+    early = [
+        pltpu.make_async_copy(a, b, early_sem.at[i])
+        for i, (a, b) in enumerate(((xt, xt_out), (qt, qt_out), (kp, kp_out), (vte, vte_out)))
+    ]
+    for c in early:
+        c.start()
 
     def score_block(h, c, place, rows, sl):
         hs = slice(h * HEAD, (h + 1) * HEAD)
@@ -252,6 +401,25 @@
             device_id=(me_dp, to), device_id_type=MESH,
         )
 
+    def late(what, h):
+        a, b = ((ut, ut_out), (p2, p2_out))[what]
+        return pltpu.make_async_copy(a.at[h], b.at[h], late_sem.at[what, h])
+
+    def keep_p(h, c, act):
+        @pl.when(c < full)
+        def _():
+            rows = pl.ds(pl.multiple_of(c * own, own), own)
+            act(pltpu.make_async_copy(pbuf.at[h, rows], p.at[h, rows], psem.at[h, c]))
+
+        @pl.when(c == full)
+        def _():
+            rows = pl.ds(full * own, rest)
+            act(pltpu.make_async_copy(pbuf.at[h, rows], p.at[h, rows], psem.at[h, c]))
+
+    pump = [
+        (1, 0, 2, 0), (1, 0, 2, 1), (3, 1, 0, 0), (5, 1, 0, 1), (8, 1, 1, 0), (9, 2, 0, 0),
+        (10, 1, 1, 1), (11, 1, 2, 0),
+    ]
     for h in range(heads):
         sl = slope[h]
 
@@ -268,15 +436,27 @@
                 score_block(h, c, 0, rest, sl)
                 short_block(h, c, sl)
 
+            keep_p(h, c, lambda copy: copy.start())
+
             @pl.when(j < n_mp - 1)
             def _():
                 out_copy(h, j + 1).start()
 
+            for when, step, stage, half in pump:
+                if when // n_mp == h:
+
+                    @pl.when(j == when % n_mp)
+                    def _():
+                        both_ways(step, stage, half)
+
             return 0
 
         lax.fori_loop(0, n_mp, chunk, 0)
-        pltpu.make_async_copy(pbuf.at[h], p.at[h], psem.at[h]).start()
-
+        late(0, h).start()
+        late(1, h).start()
+
+    for step, stage, half in ((1, 2, 1), (2, 0, 1), (2, 1, 0), (2, 2, 0), (2, 1, 1), (2, 2, 1)):
+        both_ways(step, stage, half)
     attnt[me] = obuf[me]
     for h in range(heads):
         hs = slice(h * HEAD, (h + 1) * HEAD)
@@ -286,16 +466,31 @@
     for h in range(heads):
         for j in range(1, n_mp):
             out_copy(h, j).wait_send()
-        pltpu.make_async_copy(pbuf.at[h], p.at[h], psem.at[h]).wait()
-    for c in send1 + sendw + send2:
+        for c in range(n_mp):
+            keep_p(h, c, lambda copy: copy.wait())
+        late(0, h).wait()
+        late(1, h).wait()
+    for c in early:
+        c.wait()
+    for c in send1 + send2:
         c.wait_send()
     for step in range(n_mp - 1):
-        for k in range(PIECES):
-            for way in range(2):
-
-                @pl.when(sends(way, step))
-                def _():
-                    hidden(way, step, k).wait_send()
+        for way in range(2):
+
+            @pl.when(sends(way, step))
+            def _():
+                if step < n_mp - 2:
+                    for k in range(PIECES):
+                        hidden(way, step, k).wait_send()
+                for m in range(4):
+                    weight_z(way, step, m).wait_send()
+
+    weight_stage(0, 3, 1)
+    for half in range(2):
+        weight_stage(0, 4, half)
+        for step in range(n_mp - 1):
+            both_ways(step, 3, half)
+            both_ways(step, 4, half)
 
 
 def back(
@@ -799,13 +994,13 @@
 
     attn_pack = jnp.concatenate([wq[0], wq[1], wq[2], w_out.T.astype(BF)], axis=1)
     pack = jnp.concatenate([w_gu.astype(BF), w_down.T.astype(BF)[None], attn_pack[None]], axis=0)
-    weights = lax.all_gather(pack, ("mp", "dp"), axis=1, tiled=True)
-    weights = weights.reshape(4, n_mp, width, ff_part)
+    n_q = n_dp // 2
+    units = 2 * n_mp - 1
 
     slopes = head_slopes(mp_rank * heads, heads)
     dma = pltpu.SemaphoreType.DMA
 
-    small, xt, qt, kp, vte, ut, attn, p, p2 = pl.pallas_call(
+    small, xt, qt, kp, vte, ut, attn, p, p2, weights = pl.pallas_call(
         functools.partial(front, n_dp, n_mp),
         out_shape=(
             sds((srows, width), F32),
@@ -817,12 +1012,21 @@
             sds((n_mp, cols, own), BF),
             sds((heads, LONGEST, LONGEST), BF),
             sds((heads, tail, tail), BF),
+            sds((4, n_mp, n_q, 2, wrows, ff_part), BF),
         ),
         in_specs=[vmem(), vmem(), vmem(), smem(), smem()],
-        out_specs=(vmem(), vmem(), vmem(), vmem(), vmem(), vmem(), vmem(), hbm(), vmem()),
+        out_specs=(
+            vmem(), hbm(), hbm(), hbm(), hbm(), hbm(), vmem(), hbm(), hbm(), hbm(),
+        ),
         scratch_shapes=[
+            pltpu.VMEM((width, group), BF),
+            pltpu.VMEM((cols, group), BF),
+            pltpu.VMEM((heads, group, 2 * HEAD), BF),
+            pltpu.VMEM((heads, 2 * HEAD, group), BF),
+            pltpu.VMEM((heads, 2 * HEAD, group), F32),
+            pltpu.VMEM((heads, tail, tail), BF),
             pltpu.VMEM((n_mp, own, width), BF),
-            pltpu.VMEM((n_dp, 3, wrows, cols), BF),
+            pltpu.VMEM((n_q, 2, wrows, ff_part), BF),
             pltpu.VMEM((3, width, cols), F32),
             pltpu.VMEM((3, width, cols), BF),
             pltpu.VMEM((n_mp, srows, width), F32),
@@ -838,20 +1042,28 @@
             pltpu.VMEM((n_mp, cols, own), BF),
             dma((2, n_mp - 1, PIECES)),
             dma((2, n_mp - 1, PIECES)),
-            dma((n_dp,)),
-            dma((n_dp,)),
             dma((n_mp,)),
             dma((n_mp,)),
             dma((n_dp,)),
             dma((n_dp,)),
             dma((heads, n_mp)),
             dma((heads, n_mp)),
-            dma((heads,)),
+            dma((heads, n_mp)),
+            dma((2,)),
+            dma((4,)),
+            dma((2, heads)),
+            dma((2, n_mp - 1, 4)),
+            dma((2, n_mp - 1, 4)),
+            dma((units, 4, n_q)),
+            dma((units, 4, n_q)),
+            dma((units, 2, n_q)),
+            dma((units, 2, n_q)),
         ],
         compiler_params=params(collective_id=0, has_side_effects=True),
         cost_estimate=cost(11 * LONGEST * LONGEST * HEAD * heads * 12),
         name="front",
-    )(hidden_in, wq, small_own, slopes, lengths)
+    )(hidden_in, pack, small_own, slopes, lengths)
+    weights = weights.reshape(4, n_mp, width, ff_part)
 
     fixed = lambda *s: pl.BlockSpec(s, lambda i: (0,) * len(s))
     walk = lambda i: jnp.where(i < n_mp, i, 2 * n_mp - 1 - i)
@@ -903,7 +1115,6 @@
         name="middle",
     )(attn, hidden_in, cotangent, weights, small, weights)
 
-    n_q = n_dp // 2
     gw = gw.reshape(n_mp, 3, n_q, 2, wrows, ff_part)
     gwout = gwout.reshape(n_mp, 1, n_q, 2, wrows, cols)
     grad_in, gqkv, gsmall, gff, gout = pl.pallas_call(

time: 370 us -> 326 us (0.88)
  Pallas kernels: 319 us -> 302 us
  waiting for transfers between devices: 13.6 us -> 0 us
  between operations: 14.6 us -> 1.06 us
    pallas_call x1, Pallas kernels: 152 us -> 135 us  [per_device(): pl.pallas_call(functools.partial(front, n_dp, n_mp), out_shape=(sds((srow...]
    all_gather x1 -> x0, waiting for transfers between devices: 13.5 us -> none  [per_device(): weights = lax.all_gather(pack, ('mp', 'dp'), axis=1, tiled=True)]
  transfers between devices with their start and end apart: 1 -> 0, of which waited for: 1 -> 0; matrix products, arithmetic and copies ran while one was open for 0% -> 0% of each run, Pallas kernels for 42% -> 0%
where the time goes in v3:
time: 326 us; the launch traced here: 320 us
  Pallas kernels  302 us (93%)
  local copies, waits for them, and re-layouts  12.3 us (4%)
  other arithmetic  5.2 us (2%)
    pallas_call x1, Pallas kernels, per_device(): pl.pallas_call(functools.partial(front, n_dp, n_mp), out_shape=(sds((srow...  135 us
    pallas_call x1, Pallas kernels, per_device(): pl.pallas_call(functools.partial(back, n_dp, n_mp), out_shape=(sds((own,...  126 us
    pallas_call x1, Pallas kernels, per_device(): pl.pallas_call(middle, grid=(2 * n_mp,), out_shape=(sds((own, width), BF)...  41.2 us

profile of v3, /device:TPU:0, one launch (start us, length us, event | category | flops | bytes accessed | tf_op | source)
XLA Modules:
  0.0 320.3 jit_solution(12514719061153137308)
XLA Ops:
  0.6 0.0 copy-start.1
  0.7 0.0 copy-start.2
  0.7 0.0 copy-start.3
  0.7 0.0 copy-start.4
  0.7 0.0 copy-start.5
  0.7 0.0 copy-start.6
  0.7 0.0 copy-start.7
  0.7 0.0 copy-start.8
  0.7 1.0 copy.32
  1.8 1.0 convert_element_type.25
  2.8 0.1 maximum_bitcast_fusion
  2.9 1.0 convert_bitcast_fusion
  3.9 1.1 convert_element_type.22
  5.0 0.9 pad_maximum_fusion.pack
  5.9 0.0 copy-done.1
  5.9 0.2 dynamic_update_slice.7
  6.1 0.0 copy-done.2
  6.1 0.0 copy-done.3
  6.1 0.0 copy-done.4
  6.1 0.0 copy-done.5
  6.1 0.0 copy-done.6
  6.1 0.0 copy-done.7
  6.1 0.0 copy-done.8
  6.2 0.3 dynamic_update_slice.6
  6.4 0.6 pad_maximum_fusion.1.sin
  7.1 0.5 multiply_exponential_fusion.slope
  7.6 134.6 %front.1 = (f32[16,768]{1,0:T(8,128)}, bf16[768,2048]{1,0:T(8,128)(2,1)}, bf16[192,2048]{1,0:T(8,128)(2,1)}, bf16[3,2048,128]{2,1,0:T(8,128)(2,1)}, bf16[3,128,2...) custom-call(bf16[512,768]{1,0:T(8,128)(2,1)} %x.3, ...), custom_call_target="tpu_custom_call" | custom-call | flops 70174900224 | bytes 16777216 | tf_op jit(solution)/shard_map/front/pallas_call | solution.py:1003
  142.2 41.2 %middle.1 = (bf16[512,768]{1,0:T(8,128)(2,1)}, f32[512,768]{1,0:T(8,128)}, bf16[4,192,512]{2,1,0:T(8,128)(2,1)}, bf16[4,3,768,768]{3,2,1,0:T(8,128)(2,1)}, bf16[...) custom-call(bf16[4,192,512]{2,1,0:T(8,128)(2,1)} %get-tuple-element.35.attn, bf16[512,768]{1,0:T(8,128)(2,1)} %x.3, ...), custom_call_target="tpu_custom_call" | custom-call | tf_op jit(solution)/shard_map/middle/pallas_call | solution.py:1071
  183.3 126.0 %back.1 = (bf16[512,768]{1,0:T(8,128)(2,1)}, f32[96,576]{1,0:T(8,128)}, f32[16,768]{1,0:T(8,128)}, f32[3,96,768]{2,1,0:T(8,128)}, f32[1,96,192]{2,1,0:T(8,128)}) custom-call(bf16[4,192,512]{2,1,0:T(8,128)(2,1)} %get-tuple-element.39.gt, bf16[768,2048]{1,0:T(8,128)(2,1)} %get-tuple-element.40.xt, bf16[192,2048]{1,0:T(8,128)(2,1)} %get-tuple-element.41.qt, ...), custom_call_target="tpu_custom_call" | custom-call | flops 70174900224 | bytes 16777216 | tf_op jit(solution)/shard_map/back/pallas_call | solution.py:1120
  309.3 0.0 copy-start
  309.3 1.2 copy.33
  310.5 0.9 copy.34
  311.3 0.8 fusion.1
  312.1 0.1 constant_dynamic-slice_fusion.1
  312.2 0.6 slice.46
  312.7 1.6 copy.35
  314.4 0.5 slice_bitcast_fusion.4
  314.9 1.9 slice.50
  316.9 0.6 constant_dynamic-slice_fusion
  317.5 1.7 slice_bitcast_fusion
  319.2 0.0 copy-done
  319.2 0.9 copy.39
  (6 shorter events, 0.1 us)
Async XLA Ops:
  0.6 5.2 %copy-start.1 = (f32[2,96]{1,0:T(2,128)S(1)}, f32[2,96]{1,0:T(2,128)}, u32[]{:S(2)}) copy-start(f32[2,96]{1,0:T(2,128)} %param.24) | copy-start | bytes 2308
  0.7 5.4 %copy-start.2 = (f32[2,24]{1,0:T(2,128)S(1)}, f32[2,24]{1,0:T(2,128)}, u32[]{:S(2)}) copy-start(f32[2,24]{1,0:T(2,128)} %param.18) | copy-start | bytes 580
  0.7 5.4 %copy-start.3 = (f32[24]{0:T(128)S(1)}, f32[24]{0:T(128)}, u32[]{:S(2)}) copy-start(f32[24]{0:T(128)} %param.20) | copy-start | bytes 292
  0.7 5.4 %copy-start.4 = (f32[24]{0:T(128)S(1)}, f32[24]{0:T(128)}, u32[]{:S(2)}) copy-start(f32[24]{0:T(128)} %param.21) | copy-start | bytes 292
  0.7 5.4 %copy-start.5 = (f32[24]{0:T(128)S(1)}, f32[24]{0:T(128)}, u32[]{:S(2)}) copy-start(f32[24]{0:T(128)} %param.22) | copy-start | bytes 292
  0.7 5.4 %copy-start.6 = (f32[24]{0:T(128)S(1)}, f32[24]{0:T(128)}, u32[]{:S(2)}) copy-start(f32[24]{0:T(128)} %param.26) | copy-start | bytes 292
  0.7 5.4 %copy-start.7 = (f32[24]{0:T(128)S(1)}, f32[24]{0:T(128)}, u32[]{:S(2)}) copy-start(f32[24]{0:T(128)} %param.27) | copy-start | bytes 292
  0.7 5.4 %copy-start.8 = (f32[24]{0:T(128)S(1)}, f32[24]{0:T(128)}, u32[]{:S(2)}) copy-start(f32[24]{0:T(128)} %param.28) | copy-start | bytes 292
  309.3 9.9 %copy-start = (bf16[512,768]{1,0:T(8,128)(2,1)S(1)}, bf16[512,768]{1,0:T(8,128)(2,1)}, u32[]{:S(2)}) copy-start(bf16[512,768]{1,0:T(8,128)(2,1)} %get-tuple-element.110) | copy-start | bytes 2359300

commit v4 on v3

--- a/solution.py
+++ b/solution.py
@@ -39,7 +39,7 @@
 PIECES = 4
 
 
-def greet(n_dp, n_mp, me_dp, me_mp):
+def greet(n_dp, n_mp, me_dp, me_mp, meanwhile=lambda: None):
     barrier = pltpu.get_barrier_semaphore()
     for j in range(1, n_mp):
         pl.semaphore_signal(
@@ -49,14 +49,15 @@
         pl.semaphore_signal(
             barrier, 1, device_id=(lax.rem(me_dp + j, n_dp), me_mp), device_id_type=MESH
         )
+    meanwhile()
     pl.semaphore_wait(barrier, n_mp - 1 + n_dp - 1)
 
 
 def front(
     n_dp, n_mp,
-    x, pack, sin, slope, length,
+    x, wqkv, wout, wgu, wdown, sin, slope, length,
     small, xt_out, qt_out, kp_out, vte_out, ut_out, attnt, p, p2_out, wall,
-    xt, qt, kp, vte, ut, p2, hid, wslot, wf, wb, slot1, ssum, slot2, bias, qs, kt, vext, dist, pbuf, obuf, land,
+    pack, xt, qt, kp, vte, ut, p2, hid, wslot, wf, wb, slot1, ssum, slot2, bias, qs, kt, vext, dist, pbuf, obuf, land,
     hs_sem, hr_sem, s1s, s1r, s2s, s2r, os_sem, or_sem, psem,
     local_sem, early_sem, late_sem, wzs, wzr, wqs, wqr, wps, wpr,
 ):
@@ -84,7 +85,14 @@
             device_id=(to, me), device_id_type=MESH,
         )
 
-    greet(n_dp, n_mp, me_dp, me)
+    def make_pack():
+        for m in range(2):
+            pack[m] = wgu[m].astype(BF)
+        pack[2] = wdown[...].astype(BF)
+        last = [wqkv[0], wqkv[1], wqkv[2], wout[...].T]
+        pack[3] = jnp.concatenate(last, axis=1).astype(BF)
+
+    greet(n_dp, n_mp, me_dp, me, make_pack)
 
     send1 = [across_mp(j, sin, slot1.at[j], s1s.at[j], s1r.at[j]) for j in range(1, n_mp)]
     send2 = [across_dp(j, ssum, slot2.at[j], s2s.at[j], s2r.at[j]) for j in range(1, n_dp)]
@@ -496,7 +504,7 @@
 def back(
     n_dp, n_mp,
     gt, xt, qt, kp, vte, ut, p, p2, weights, dsum1, sin, gw, gwo,
-    grad_in, gq, small, gff, gout,
+    grad_in, gq, small, ggu, gdown, gout,
     gl, pbuf, dkt, dvt, dbuf, dland, wfull, gbuf, qland, ssum, slot1, slot2,
     pair, cland, xland, zsum, zland, opair, ocland, oxland, ozsum, ozland,
     gs_sem, gr_sem, qs_sem, qr_sem, ds_sem, dr_sem, ws_sem, wr_sem, s1s, s1r, s2s, s2r,
@@ -510,7 +518,7 @@
     tail = group - LONGEST
     full = LONGEST // own
     rest = LONGEST - full * own
-    wrows = gq.shape[0]
+    wrows = gq.shape[1]
 
     def across_mp(j, src, dst, ss, rs):
         to = lax.rem(me + j, n_mp)
@@ -799,22 +807,28 @@
     for j in range(1, n_dp):
         weight_copy(j).wait_recv()
         total += qland[j].astype(F32)
-    gq[...] = total
+    for s in range(3):
+        gq[s] = total[:, s * cols : (s + 1) * cols]
     total = ssum[...]
     for c in send2:
         c.wait_recv()
     for j in range(1, n_dp):
         total += slot2[j]
     small[...] = total
-    for t, out in ((0, gff), (1, gout)):
+    for t in range(2):
         total, land = kinds[t][4:]
         for o in range(n_mp - 1):
             along(o, t).wait_recv()
-        for m in range(out.shape[0]):
+        for m in range(total.shape[1]):
             a = total[n_mp - 1, m].astype(F32)
             for o in range(n_mp - 1):
                 a += land[o, m].astype(F32)
-            out[m] = a
+            if t == 1:
+                gout[...] = a.T
+            elif m == 2:
+                gdown[...] = a
+            else:
+                ggu[m] = a
     for t in range(2):
         for o in range(n_mp):
             pair_up(o, t).wait_send()
@@ -947,6 +961,12 @@
             gwout[r] = dot_nt(dbt, attn[r]).astype(BF)
 
 
+def hand_on(*refs):
+    n = len(refs) // 2
+    for a, b in zip(refs[:n], refs[n:]):
+        b[...] = a[...]
+
+
 def head_slopes(first_head, head_count):
     number = first_head + jnp.arange(head_count, dtype=jnp.int32)
     exponent = jnp.where(number < 8, number.astype(F32) + 1.0, number.astype(F32) - 7.5)
@@ -986,14 +1006,11 @@
     )
     srows = small_own.shape[0]
 
-    wq = w_qkv.astype(BF)
-    wrows, cols = wq.shape[1], wq.shape[2]
+    wrows, cols = w_qkv.shape[1], w_qkv.shape[2]
     ff_part = w_gu.shape[2]
     heads = cols // HEAD
     tail = group - LONGEST
 
-    attn_pack = jnp.concatenate([wq[0], wq[1], wq[2], w_out.T.astype(BF)], axis=1)
-    pack = jnp.concatenate([w_gu.astype(BF), w_down.T.astype(BF)[None], attn_pack[None]], axis=0)
     n_q = n_dp // 2
     units = 2 * n_mp - 1
 
@@ -1014,11 +1031,12 @@
             sds((heads, tail, tail), BF),
             sds((4, n_mp, n_q, 2, wrows, ff_part), BF),
         ),
-        in_specs=[vmem(), vmem(), vmem(), smem(), smem()],
+        in_specs=[vmem(), vmem(), vmem(), vmem(), vmem(), vmem(), smem(), smem()],
         out_specs=(
             vmem(), hbm(), hbm(), hbm(), hbm(), hbm(), vmem(), hbm(), hbm(), hbm(),
         ),
         scratch_shapes=[
+            pltpu.VMEM((4, wrows, ff_part), BF),
             pltpu.VMEM((width, group), BF),
             pltpu.VMEM((cols, group), BF),
             pltpu.VMEM((heads, group, 2 * HEAD), BF),
@@ -1062,7 +1080,7 @@
         compiler_params=params(collective_id=0, has_side_effects=True),
         cost_estimate=cost(11 * LONGEST * LONGEST * HEAD * heads * 12),
         name="front",
-    )(hidden_in, pack, small_own, slopes, lengths)
+    )(hidden_in, w_qkv, w_out, w_gu, w_down.T, small_own, slopes, lengths)
     weights = weights.reshape(4, n_mp, width, ff_part)
 
     fixed = lambda *s: pl.BlockSpec(s, lambda i: (0,) * len(s))
@@ -1117,20 +1135,21 @@
 
     gw = gw.reshape(n_mp, 3, n_q, 2, wrows, ff_part)
     gwout = gwout.reshape(n_mp, 1, n_q, 2, wrows, cols)
-    grad_in, gqkv, gsmall, gff, gout = pl.pallas_call(
+    grad_in, gqkv, gsmall, ggu, gdown, gout = pl.pallas_call(
         functools.partial(back, n_dp, n_mp),
         out_shape=(
             sds((own, width), BF),
-            sds((wrows, 3 * cols), F32),
+            sds((3, wrows, cols), F32),
             sds((srows, width), F32),
-            sds((3, wrows, ff_part), F32),
-            sds((1, wrows, cols), F32),
+            sds((2, wrows, ff_part), F32),
+            sds((wrows, ff_part), F32),
+            sds((cols, wrows), F32),
         ),
         in_specs=[
             vmem(), vmem(), vmem(), vmem(), vmem(), vmem(), hbm(), vmem(), hbm(), vmem(), vmem(),
             hbm(), hbm(),
         ],
-        out_specs=(vmem(), vmem(), vmem(), vmem(), vmem()),
+        out_specs=(vmem(), vmem(), vmem(), vmem(), vmem(), vmem()),
         scratch_shapes=[
             pltpu.VMEM((n_mp, cols, own), BF),
             pltpu.VMEM((2, own, LONGEST), BF),
@@ -1181,26 +1200,35 @@
         name="back",
     )(dattn, xt, qt, kp, vte, ut, p, p2, weights, dsum1, gsmall, gw, gwout)
 
+    finished = (grad_in, gqkv, ggu, gdown, gout)
+    grad_in, gqkv, ggu, gdown, gout = pl.pallas_call(
+        hand_on,
+        out_shape=tuple(sds(a.shape, a.dtype) for a in finished),
+        in_specs=[vmem()] * len(finished),
+        out_specs=(vmem(),) * len(finished),
+        compiler_params=params(),
+        name="hand_on",
+    )(*finished)
+
     def own_columns(a):
         part = a.shape[1] // n
         return lax.dynamic_slice_in_dim(a, dev * part, part, 1)
 
     gs = own_columns(gsmall[:8])
     g_gu = own_columns(gsmall[8:].reshape(2, -1))
-    gqkv = gqkv.reshape(wrows, 3, cols).transpose(1, 0, 2)
 
     return (
         result,
         grad_in,
         gqkv,
         gs[0:2],
-        gout[0].T,
+        gout,
         gs[2],
         gs[3],
         gs[4],
-        gff[:2],
+        ggu,
         g_gu,
-        gff[2].T,
+        gdown.T,
         gs[5],
         gs[6],
         gs[7],

time: 326 us -> 317 us (0.972)
  local copies, waits for them, and re-layouts: 12.3 us -> 4.46 us
  other arithmetic: 5.2 us -> 1.15 us
    unnamed x22 -> x0, local copies, waits for them, and re-layouts: 4.45 us -> none
where the time goes in v4:
time: 317 us; the launch traced here: 311 us
  Pallas kernels  305 us (96%)
  local copies, waits for them, and re-layouts  4.46 us (1%)
    pallas_call x1, Pallas kernels, per_device(): pl.pallas_call(functools.partial(front, n_dp, n_mp), out_shape=(sds((srow...  135 us
    pallas_call x1, Pallas kernels, per_device(): pl.pallas_call(functools.partial(back, n_dp, n_mp), out_shape=(sds((own,...  126 us
    pallas_call x1, Pallas kernels, per_device(): pl.pallas_call(middle, grid=(2 * n_mp,), out_shape=(sds((own, width), BF)...  41.2 us

profile of v4, /device:TPU:0, one launch (start us, length us, event | category | flops | bytes accessed | tf_op | source)
XLA Modules:
  0.0 311.3 jit_solution(13645341324882059676)
XLA Ops:
  0.7 0.8 dynamic_update_slice.7
  1.5 0.8 concatenate.6
  2.3 0.3 dynamic_update_slice.6
  2.5 0.6 pad_maximum_fusion.sin
  3.2 0.5 multiply_exponential_fusion.slope
  3.7 134.8 %front.1 = (f32[16,768]{1,0:T(8,128)}, bf16[768,2048]{1,0:T(8,128)(2,1)}, bf16[192,2048]{1,0:T(8,128)(2,1)}, bf16[3,2048,128]{2,1,0:T(8,128)(2,1)}, bf16[3,128,2...) custom-call(bf16[512,768]{1,0:T(8,128)(2,1)} %x.3, ...), custom_call_target="tpu_custom_call" | custom-call | flops 70174900224 | bytes 16777216 | tf_op jit(solution)/shard_map/front/pallas_call | solution.py:1020
  138.5 41.2 %middle.1 = (bf16[512,768]{1,0:T(8,128)(2,1)}, f32[512,768]{1,0:T(8,128)}, bf16[4,192,512]{2,1,0:T(8,128)(2,1)}, bf16[4,3,768,768]{3,2,1,0:T(8,128)(2,1)}, bf16[...) custom-call(bf16[4,192,512]{2,1,0:T(8,128)(2,1)} %get-tuple-element.41.attn, bf16[512,768]{1,0:T(8,128)(2,1)} %x.3, ...), custom_call_target="tpu_custom_call" | custom-call | tf_op jit(solution)/shard_map/middle/pallas_call | solution.py:1089
  179.7 126.0 %back.1 = (bf16[512,768]{1,0:T(8,128)(2,1)}, f32[3,96,192]{2,1,0:T(8,128)}, f32[16,768]{1,0:T(8,128)}, f32[2,96,768]{2,1,0:T(8,128)}, f32[96,768]{1,0:T(8,128)}, /*index=5*/f32[192,96]{1,0:T(8,128)}) custom-call(bf16[4,192,512]{2,1,0:T(8,128)(2,1)} %get-tuple-element.45.gt, bf16[768,2048]{1,0:T(8,128)(2,1)} %get-tuple-element.46.xt, ...), custom_call_target="tpu_custom_call" | custom-call | flops 70174900224 | bytes 16777216 | tf_op jit(solution)/shard_map/back/pallas_call | solution.py:1138
  305.7 2.8 hand_on.1
  308.5 0.8 fusion.1
  309.3 0.1 constant_dynamic-slice_fusion.1
  309.3 0.6 slice.28
  309.9 0.5 slice_bitcast_fusion
  310.5 0.6 constant_dynamic-slice_fusion
  (4 shorter events, 0.0 us)

commit v5 on v4

--- a/solution.py
+++ b/solution.py
@@ -425,8 +425,9 @@
             act(pltpu.make_async_copy(pbuf.at[h, rows], p.at[h, rows], psem.at[h, c]))
 
     pump = [
-        (1, 0, 2, 0), (1, 0, 2, 1), (3, 1, 0, 0), (5, 1, 0, 1), (8, 1, 1, 0), (9, 2, 0, 0),
-        (10, 1, 1, 1), (11, 1, 2, 0),
+        (0, 0, 2, 0), (0, 1, 0, 0), (1, 0, 2, 1), (1, 1, 0, 1), (3, 1, 1, 0), (4, 2, 0, 0),
+        (5, 1, 1, 1), (6, 2, 0, 1), (7, 1, 2, 0), (8, 1, 2, 1), (9, 2, 1, 0), (10, 2, 1, 1),
+        (11, 2, 2, 0),
     ]
     for h in range(heads):
         sl = slope[h]
@@ -463,8 +464,7 @@
         late(0, h).start()
         late(1, h).start()
 
-    for step, stage, half in ((1, 2, 1), (2, 0, 1), (2, 1, 0), (2, 2, 0), (2, 1, 1), (2, 2, 1)):
-        both_ways(step, stage, half)
+    both_ways(2, 2, 1)
     attnt[me] = obuf[me]
     for h in range(heads):
         hs = slice(h * HEAD, (h + 1) * HEAD)

time: 317 us -> 309 us (0.975)
  Pallas kernels: 305 us -> 297 us
    pallas_call x1, Pallas kernels: 135 us -> 127 us  [per_device(): pl.pallas_call(functools.partial(front, n_dp, n_mp), out_shape=(sds((srow...]
where the time goes in v5:
time: 309 us; the launch traced here: 304 us
  Pallas kernels  297 us (96%)
  local copies, waits for them, and re-layouts  4.46 us (1%)
    pallas_call x1, Pallas kernels, per_device(): pl.pallas_call(functools.partial(front, n_dp, n_mp), out_shape=(sds((srow...  127 us
    pallas_call x1, Pallas kernels, per_device(): pl.pallas_call(functools.partial(back, n_dp, n_mp), out_shape=(sds((own,...  126 us
    pallas_call x1, Pallas kernels, per_device(): pl.pallas_call(middle, grid=(2 * n_mp,), out_shape=(sds((own, width), BF)...  41.2 us

profile of v5, /device:TPU:0, one launch (start us, length us, event | category | flops | bytes accessed | tf_op | source)
XLA Modules:
  0.0 303.9 jit_solution(3245358965609141837)
XLA Ops:
  0.7 0.8 dynamic_update_slice.7
  1.5 0.8 concatenate.6
  2.3 0.3 dynamic_update_slice.6
  2.5 0.6 pad_maximum_fusion.sin
  3.2 0.5 multiply_exponential_fusion.slope
  3.7 127.4 %front.1 = (f32[16,768]{1,0:T(8,128)}, bf16[768,2048]{1,0:T(8,128)(2,1)}, bf16[192,2048]{1,0:T(8,128)(2,1)}, bf16[3,2048,128]{2,1,0:T(8,128)(2,1)}, bf16[3,128,2...) custom-call(bf16[512,768]{1,0:T(8,128)(2,1)} %x.3, ...), custom_call_target="tpu_custom_call" | custom-call | flops 70174900224 | bytes 16777216 | tf_op jit(solution)/shard_map/front/pallas_call | solution.py:1020
  131.1 41.2 %middle.1 = (bf16[512,768]{1,0:T(8,128)(2,1)}, f32[512,768]{1,0:T(8,128)}, bf16[4,192,512]{2,1,0:T(8,128)(2,1)}, bf16[4,3,768,768]{3,2,1,0:T(8,128)(2,1)}, bf16[...) custom-call(bf16[4,192,512]{2,1,0:T(8,128)(2,1)} %get-tuple-element.41.attn, bf16[512,768]{1,0:T(8,128)(2,1)} %x.3, ...), custom_call_target="tpu_custom_call" | custom-call | tf_op jit(solution)/shard_map/middle/pallas_call | solution.py:1089
  172.3 126.0 %back.1 = (bf16[512,768]{1,0:T(8,128)(2,1)}, f32[3,96,192]{2,1,0:T(8,128)}, f32[16,768]{1,0:T(8,128)}, f32[2,96,768]{2,1,0:T(8,128)}, f32[96,768]{1,0:T(8,128)}, /*index=5*/f32[192,96]{1,0:T(8,128)}) custom-call(bf16[4,192,512]{2,1,0:T(8,128)(2,1)} %get-tuple-element.45.gt, bf16[768,2048]{1,0:T(8,128)(2,1)} %get-tuple-element.46.xt, ...), custom_call_target="tpu_custom_call" | custom-call | flops 70174900224 | bytes 16777216 | tf_op jit(solution)/shard_map/back/pallas_call | solution.py:1138
  298.3 2.8 hand_on.1
  301.1 0.8 fusion.1
  301.9 0.1 constant_dynamic-slice_fusion.1
  302.0 0.6 slice.28
  302.5 0.5 slice_bitcast_fusion
  303.1 0.6 constant_dynamic-slice_fusion
  (4 shorter events, 0.0 us)

commit v6 on v5

--- a/solution.py
+++ b/solution.py
@@ -687,7 +687,7 @@
             dkt[:, keys] = dk
             dvt[:, keys] = dv
 
-    pump = [1 + o for o in range(n_mp)]
+    pump = [o for o in range(n_mp)]
     for h in range(heads):
         hs = slice(h * HEAD, (h + 1) * HEAD)
         dkt[:, :LONGEST] = jnp.zeros((HEAD, LONGEST), F32)

time: 309 us -> 309 us (level)
  no operation moved by 1% of the time
where the time goes in v6:
time: 309 us; the launch traced here: 304 us
  Pallas kernels  297 us (96%)
  local copies, waits for them, and re-layouts  4.46 us (1%)
    pallas_call x1, Pallas kernels, per_device(): pl.pallas_call(functools.partial(front, n_dp, n_mp), out_shape=(sds((srow...  127 us
    pallas_call x1, Pallas kernels, per_device(): pl.pallas_call(functools.partial(back, n_dp, n_mp), out_shape=(sds((own,...  126 us
    pallas_call x1, Pallas kernels, per_device(): pl.pallas_call(middle, grid=(2 * n_mp,), out_shape=(sds((own, width), BF)...  41.2 us

profile of v6, /device:TPU:0, one launch (start us, length us, event | category | flops | bytes accessed | tf_op | source)
XLA Modules:
  0.0 303.9 jit_solution(3962858465598880812)
XLA Ops:
  0.7 0.8 dynamic_update_slice.7
  1.5 0.8 concatenate.6
  2.3 0.3 dynamic_update_slice.6
  2.5 0.6 pad_maximum_fusion.sin
  3.2 0.5 multiply_exponential_fusion.slope
  3.7 127.4 %front.1 = (f32[16,768]{1,0:T(8,128)}, bf16[768,2048]{1,0:T(8,128)(2,1)}, bf16[192,2048]{1,0:T(8,128)(2,1)}, bf16[3,2048,128]{2,1,0:T(8,128)(2,1)}, bf16[3,128,2...) custom-call(bf16[512,768]{1,0:T(8,128)(2,1)} %x.3, ...), custom_call_target="tpu_custom_call" | custom-call | flops 70174900224 | bytes 16777216 | tf_op jit(solution)/shard_map/front/pallas_call | solution.py:1020
  131.1 41.2 %middle.1 = (bf16[512,768]{1,0:T(8,128)(2,1)}, f32[512,768]{1,0:T(8,128)}, bf16[4,192,512]{2,1,0:T(8,128)(2,1)}, bf16[4,3,768,768]{3,2,1,0:T(8,128)(2,1)}, bf16[...) custom-call(bf16[4,192,512]{2,1,0:T(8,128)(2,1)} %get-tuple-element.41.attn, bf16[512,768]{1,0:T(8,128)(2,1)} %x.3, ...), custom_call_target="tpu_custom_call" | custom-call | tf_op jit(solution)/shard_map/middle/pallas_call | solution.py:1089
  172.3 126.0 %back.1 = (bf16[512,768]{1,0:T(8,128)(2,1)}, f32[3,96,192]{2,1,0:T(8,128)}, f32[16,768]{1,0:T(8,128)}, f32[2,96,768]{2,1,0:T(8,128)}, f32[96,768]{1,0:T(8,128)}, /*index=5*/f32[192,96]{1,0:T(8,128)}) custom-call(bf16[4,192,512]{2,1,0:T(8,128)(2,1)} %get-tuple-element.45.gt, bf16[768,2048]{1,0:T(8,128)(2,1)} %get-tuple-element.46.xt, ...), custom_call_target="tpu_custom_call" | custom-call | flops 70174900224 | bytes 16777216 | tf_op jit(solution)/shard_map/back/pallas_call | solution.py:1138
  298.3 2.8 hand_on.1
  301.1 0.8 fusion.1
  301.9 0.1 constant_dynamic-slice_fusion.1
  302.0 0.6 slice.28
  302.5 0.5 slice_bitcast_fusion
  303.1 0.6 constant_dynamic-slice_fusion
  (4 shorter events, 0.0 us)
